TPU v7x, 256 devices: a whole 4x4x8 slice. The times are simulated.
256 devices in a mesh: ka: 16 (over z, y_lo), pb: 16 (over y_hi, x, core).
Axes of the slice: x: 4, y: 4 (y_hi: 2, y_lo: 2; y = y_hi * 2 + y_lo), z: 8, core: 2. Of those that a mesh axis runs over, the one named last changes fastest.
Arguments:
- dipole: float32 [16, 4096], P('ka', 'pb'), may hold values from -400 to 400
- energy: float32 [16, 4096], P('ka', 'pb'), may hold values from 1 to 4
- cond_amp: bfloat16 [16, 64, 2048], P('ka', None, 'pb'), may hold values from -6 to 6
- val_amp: bfloat16 [16, 64, 2048], P('pb', None, 'ka'), may hold values from -6 to 6
- screened: bfloat16 [128, 2048, 2048], P('pb', None, 'ka'), may hold values from -6 to 6
- window: int32 [16], replicated, may hold values from 0 to 127, as said below
Outputs:
- coefficients: float32 [4], replicated
- last_vector: float32 [16, 4096], P('ka', 'pb')
Inputs may be any that keep to these rules, and one draw needn't show every extreme that they name: `window`: distinct grid indices; the first two are 0 and 127.
All inputs are finite; a program needn't handle non-finite values.
Results may differ from a plain program's by a relative error of at most 0.018.
Values may be sent and summed in bfloat16 or wider, within the bound.
A program may use at most 64 MiB of HBM per device.

v0:
```python
import math

import jax
import jax.numpy as jnp
from jax import lax
from jax.sharding import PartitionSpec as P

NC = 64
NV = 64
NG = 2048
ITERS = 2
GX = 4
GY = 8


EPSILON = 1e-06


def q_table(window, q_count):
    third_len = q_count // (GX * GY)
    coord_one = window // (GY * third_len)
    coord_two = window // third_len % GY
    coord_three = window % third_len
    shift_one = jnp.remainder(coord_one[:, None] - coord_one[None, :], GX)
    shift_two = jnp.remainder(coord_two[:, None] - coord_two[None, :], GY)
    shift_three = jnp.remainder(coord_three[:, None] - coord_three[None, :], third_len)
    return (shift_one * GY + shift_two) * third_len + shift_three


def kernel_block(full_vector, cond_all, val_all, blocks, q_index):
    point_count = full_vector.shape[0]
    vec_half = full_vector.reshape(point_count, NC, NV)
    half_prod = jnp.einsum(
        "kcv,kvh->kch", vec_half, val_all, preferred_element_type=jnp.float32
    ).astype(jnp.bfloat16)
    pair_dens = jnp.einsum(
        "kcg,kch->kgh", cond_all, half_prod, preferred_element_type=jnp.float32
    ).astype(jnp.bfloat16)
    group_size = math.gcd(point_count, 8)
    group_count = point_count // group_size
    q_groups = q_index.reshape(group_count, group_size, point_count)
    cond_groups = cond_all.reshape(group_count, group_size, NC, cond_all.shape[2])
    val_groups = val_all.reshape(group_count, group_size, NV, val_all.shape[2])

    def per_group(inputs):
        q_rows, cond_part, val_part = inputs
        picked = jnp.take(blocks, q_rows, axis=0)
        summed = jnp.einsum(
            "jkgh,kgh->jgh", picked, pair_dens, preferred_element_type=jnp.float32
        ).astype(jnp.bfloat16)
        projected = jnp.einsum("jgh,jvh->jgv", summed, val_part, preferred_element_type=jnp.float32)
        result = jnp.einsum(
            "jcg,jgv->jcv",
            cond_part.astype(jnp.float32),
            projected,
            precision=lax.Precision.HIGHEST,
        )
        return result.reshape(group_size, NC * NV)

    return lax.map(per_group, (q_groups, cond_groups, val_groups)).reshape(point_count, NC * NV)


def per_device(dipole, energy, cond_amp, val_amp, screened, window):
    cond_all = lax.all_gather(cond_amp, "ka", axis=0, tiled=True)
    val_all = lax.all_gather(val_amp, "pb", axis=0, tiled=True)
    blocks = lax.all_to_all(screened, "pb", split_axis=1, concat_axis=0, tiled=True)
    q_index = q_table(window, blocks.shape[0])
    point_count = window.shape[0]
    entries = point_count * NC * NV
    factor = 1.0 / (NG * math.sqrt(entries))
    alpha_list = []
    beta_list = []
    beta_now = jnp.zeros((), jnp.float32)
    start_sum = lax.psum(jnp.sum(dipole * dipole), ("ka", "pb"))
    vector = dipole / jnp.sqrt(start_sum / entries + EPSILON)
    former = jnp.zeros_like(vector)
    for iteration in range(ITERS):
        cols_full = lax.all_gather(vector.astype(jnp.bfloat16), "pb", axis=1, tiled=True)
        full_vector = lax.all_gather(cols_full, "ka", axis=0, tiled=True)
        kernel_part = kernel_block(full_vector, cond_all, val_all, blocks, q_index)
        row_part = lax.psum_scatter(kernel_part, "ka", scatter_dimension=0, tiled=True)
        kernel_out = lax.psum_scatter(row_part, "pb", scatter_dimension=1, tiled=True)
        image_vec = energy * vector - factor * kernel_out
        alpha_now = lax.psum(jnp.sum(vector * image_vec), ("ka", "pb")) / entries
        residual = image_vec - alpha_now * vector - beta_now * former
        square = lax.psum(jnp.sum(residual * residual), ("ka", "pb")) / entries
        beta_now = jnp.sqrt(square + EPSILON)
        former = vector
        vector = residual / beta_now
        alpha_list.append(alpha_now)
        beta_list.append(beta_now)
    coefficients = jnp.stack(alpha_list + beta_list)
    return (coefficients, vector)


def solution(mesh):
    in_specs = (
        P("ka", "pb"),
        P("ka", "pb"),
        P("ka", None, "pb"),
        P("pb", None, "ka"),
        P("pb", None, "ka"),
        P(),
    )
    out_specs = (P(), P("ka", "pb"))
    return jax.shard_map(
        per_device, mesh=mesh, in_specs=in_specs, out_specs=out_specs, check_vma=False
    )
```

profile of v0, /device:TPU:1, one launch (start us, length us, event | category | flops | bytes accessed | tf_op | source)
XLA Modules:
  0.0 1099.6 jit_solution(10594349405803055023)
XLA Ops:
  7.2 6.2 copy.14
  13.3 8.6 all-to-all-start
  22.0 0.6 multiply_reduce_fusion.6
  22.6 125.4 %psum.35 = f32[]{:T(128)} all-reduce(f32[]{:T(128)} %multiply_reduce_fusion.6), channel_id=1, replica_groups=mesh['ka'=16,'pb'=16] {'ka','pb'}, use_global_device_ids=true, to_apply=%region_1.2 | all-reduce | flops 1 | bytes 8 | tf_op jit(solution)/shard_map/psum | solution.py:74
  149.0 21.9 %all_gather.19 = bf16[1,4096]{1,0:T(2,128)(2,1)S(1)} all-gather(bf16[1,256]{1,0:T(2,128)(2,1)S(1)} %get-tuple-element.159), channel_id=1, replica_groups=mesh['ka'=16,'pb'=16] {'pb'}, dimensions={1}, use_global_device_ids=true | all-gather | bytes 8704 | tf_op jit(solution)/shard_map/all_gather | solution.py:78
  170.9 25.0 %all-gather = bf16[16,1,4096]{2,1,0:T(2,128)(2,1)S(1)} all-gather(bf16[1,1,4096]{2,1,0:T(2,128)(2,1)S(1)} %bitcast.106), channel_id=1, replica_groups=mesh['ka'=16,'pb'=16] {'ka'}, dimensions={0}, use_global_device_ids=true | all-gather | bytes 139264 | tf_op jit(solution)/shard_map/all_gather | solution.py:79
  195.9 0.7 reduce.2
  196.9 25.4 %all_gather.18 = bf16[16,64,128]{2,1,0:T(8,128)(2,1)S(1)} all-gather(bf16[1,64,128]{2,1,0:T(8,128)(2,1)S(1)} %copy-done.2), channel_id=1, replica_groups=mesh['ka'=16,'pb'=16] {'ka'}, dimensions={0}, use_global_device_ids=true | all-gather | bytes 278528 | tf_op jit(solution)/shard_map/all_gather | solution.py:64
  222.3 33.6 %all_gather.21 = bf16[16,64,128]{2,1,0:T(8,128)(2,1)S(1)} all-gather(bf16[1,64,128]{2,1,0:T(8,128)(2,1)S(1)} %copy-done.3), channel_id=1, replica_groups=mesh['ka'=16,'pb'=16] {'pb'}, dimensions={0}, use_global_device_ids=true | all-gather | bytes 278528 | tf_op jit(solution)/shard_map/all_gather | solution.py:65
  255.9 0.5 fusion.20
  256.7 5.4 copy.15
  262.1 18.6 %while.20 = (s32[]{:T(128)}, f32[2,8,4096]{2,1,0:T(8,128)S(1)}, bf16[2,8,64,128]{3,2,1,0:T(8,128)(2,1)S(1)}, s32[2,8,16]{2,1,0:T(8,128)S(1)}, bf16[128,128,128]{...) while((s32[]{:T(128)}, f32[2,8,4096]{2,1,0:T(8,128)S(1)}, ...), condition=%wide.region_3.5_spmd, body=%wide.region_2.4_spmd.sunk | while | flops 75630336 | bytes 17177956 | solution.py:60
  262.3 5.2 gather_fusion
  267.6 3.1 multiply_reduce_fusion.9
  271.6 5.2 gather_fusion
  276.9 3.1 multiply_reduce_fusion.9
  280.8 0.7 copy-done.1
  281.6 0.6 dynamic-slice
  282.2 122.0 %all-reduce.5.cloned.1.call-done = f32[16,4096]{1,0:T(8,128)} async-done(((f32[16,4096]{1,0:T(8,128)}), f32[16,4096]{1,0:T(8,128)}) %all-reduce.5.cloned.1.call-update) | async-done | bytes 262160
  404.2 1.6 constant_dynamic-slice_fusion.1
  405.7 2.0 copy.32
  407.8 87.8 %reduce-scatter.7.cloned.1.call-done = f32[256,1]{1,0:T(8,128)} async-done(((f32[4096,1]{1,0:T(8,128)}), f32[256,1]{1,0:T(8,128)}) %reduce-scatter.7.cloned.1.call-update) | async-done | bytes 1040
  495.6 1.0 copy.33
  496.5 0.6 multiply_reduce_fusion.5
  497.2 77.4 %psum.36 = f32[]{:T(128)} all-reduce(f32[]{:T(128)} %multiply_reduce_fusion.5), channel_id=1, replica_groups=mesh['ka'=16,'pb'=16] {'ka','pb'}, use_global_device_ids=true, to_apply=%region_7.9 | all-reduce | flops 1 | bytes 8 | tf_op jit(solution)/shard_map/psum | solution.py:84
  575.2 0.6 multiply_reduce_fusion.4
  575.8 73.4 %psum.37 = f32[]{:T(128)} all-reduce(f32[]{:T(128)} %get-tuple-element.157), channel_id=1, replica_groups=mesh['ka'=16,'pb'=16] {'ka','pb'}, use_global_device_ids=true, to_apply=%region_9.11 | all-reduce | flops 1 | bytes 8 | tf_op jit(solution)/shard_map/psum | solution.py:86
  649.9 21.5 %all_gather.22 = bf16[1,4096]{1,0:T(2,128)(2,1)S(1)} all-gather(bf16[1,256]{1,0:T(2,128)(2,1)S(1)} %get-tuple-element.155), channel_id=1, replica_groups=mesh['ka'=16,'pb'=16] {'pb'}, dimensions={1}, use_global_device_ids=true | all-gather | bytes 8704 | tf_op jit(solution)/shard_map/all_gather | solution.py:78
  671.4 24.8 %all-gather.1 = bf16[16,1,4096]{2,1,0:T(2,128)(2,1)S(1)} all-gather(bf16[1,1,4096]{2,1,0:T(2,128)(2,1)S(1)} %bitcast.107), channel_id=1, replica_groups=mesh['ka'=16,'pb'=16] {'ka'}, dimensions={0}, use_global_device_ids=true | all-gather | bytes 139264 | tf_op jit(solution)/shard_map/all_gather | solution.py:79
  696.2 0.7 reduce.3
  697.2 0.5 fusion.21
  698.0 18.6 %while.21 = (s32[]{:T(128)}, f32[2,8,4096]{2,1,0:T(8,128)S(1)}, bf16[2,8,64,128]{3,2,1,0:T(8,128)(2,1)S(1)}, s32[2,8,16]{2,1,0:T(8,128)S(1)}, bf16[128,128,128]{...) while((s32[]{:T(128)}, f32[2,8,4096]{2,1,0:T(8,128)S(1)}, ...), condition=%wide.region_11.13_spmd, body=%wide.region_10.12_spmd.sunk | while | flops 75630336 | bytes 17177956 | solution.py:60
  698.1 5.2 gather_fusion.1
  703.4 3.1 multiply_reduce_fusion.10
  707.4 5.2 gather_fusion.1
  712.8 3.1 multiply_reduce_fusion.10
  716.6 0.7 copy-done
  717.4 129.6 %all-reduce.7.cloned.1.call-done = f32[16,4096]{1,0:T(8,128)} async-done(((f32[16,4096]{1,0:T(8,128)}), f32[16,4096]{1,0:T(8,128)}) %all-reduce.7.cloned.1.call-update) | async-done | bytes 262160
  847.0 1.6 constant_dynamic-slice_fusion
  848.5 2.0 copy.34
  850.6 87.1 %reduce-scatter.9.cloned.1.call-done = f32[256,1]{1,0:T(8,128)} async-done(((f32[4096,1]{1,0:T(8,128)}), f32[256,1]{1,0:T(8,128)}) %reduce-scatter.9.cloned.1.call-update) | async-done | bytes 1040
  937.6 1.0 copy.35
  938.6 0.6 multiply_reduce_fusion.3
  939.2 77.4 %psum.38 = f32[]{:T(128)} all-reduce(f32[]{:T(128)} %multiply_reduce_fusion.3), channel_id=1, replica_groups=mesh['ka'=16,'pb'=16] {'ka','pb'}, use_global_device_ids=true, to_apply=%region_15.17 | all-reduce | flops 1 | bytes 8 | tf_op jit(solution)/shard_map/psum | solution.py:84
  1017.3 0.6 multiply_reduce_fusion.2
  1017.9 73.4 %psum.39 = f32[]{:T(128)} all-reduce(f32[]{:T(128)} %get-tuple-element.153), channel_id=1, replica_groups=mesh['ka'=16,'pb'=16] {'ka','pb'}, use_global_device_ids=true, to_apply=%region_17.19 | all-reduce | flops 1 | bytes 8 | tf_op jit(solution)/shard_map/psum | solution.py:86
  1092.0 0.6 broadcast_divide_fusion
  1092.5 0.6 pad_maximum_fusion
  (68 shorter events, 5.5 us)
Async XLA Ops:
  13.3 8.7 copy-start.5
  13.3 134.7 %copy-start.6 = (s32[16]{0:T(128)S(1)}, s32[16]{0:T(128)}, u32[]{:S(2)}) copy-start(s32[16]{0:T(128)} %param.17) | copy-start | bytes 196
  13.3 183.6 %copy-start.2 = (bf16[1,64,128]{2,1,0:T(8,128)(2,1)S(1)}, bf16[1,64,128]{2,1,0:T(8,128)(2,1)}, u32[]{:S(2)}) copy-start(bf16[1,64,128]{2,1,0:T(8,128)(2,1)} %param.14) | copy-start | bytes 49156
  13.3 208.9 %copy-start.3 = (bf16[1,64,128]{2,1,0:T(8,128)(2,1)S(1)}, bf16[1,64,128]{2,1,0:T(8,128)(2,1)}, u32[]{:S(2)}) copy-start(bf16[1,64,128]{2,1,0:T(8,128)(2,1)} %param.15) | copy-start | bytes 49156
  13.3 243.4 %all-to-all-start = ((bf16[8,2048,128]{2,0,1:T(8,128)(2,1)}), bf16[8,2048,128]{2,0,1:T(8,128)(2,1)}, u32[]{:S(2)}, u32[]{:S(2)}) async-start(bf16[8,2048,128]{2,0,1:T(8,128)(2,1)} %copy.14), calls=%async_computation | async-start | bytes 8388608 | tf_op jit(solution)/shard_map/all_to_all | solution.py:66
  21.9 382.2 %all-reduce.5.cloned.1.call-start = ((), (), s32[]{:S(2)}) async-start(), calls=%async_computation.5 | async-start | bytes 524288
  262.1 19.4 %copy-start.7 = (u32[256]{0:T(256)S(1)}, u32[256]{0:T(256)}, u32[]{:S(2)}) copy-start(u32[256]{0:T(256)} %constant.125) | copy-start | bytes 3076
  280.8 0.7 copy-start.1
  280.8 215.7 %copy-start.4 = (f32[1,256]{1,0:T(1,128)S(1)}, f32[1,256]{1,0:T(1,128)}, u32[]{:S(2)}) copy-start(f32[1,256]{1,0:T(1,128)} %param.13) | copy-start | bytes 3076
  281.5 214.1 %reduce-scatter.7.cloned.1.call-start = ((), (), s32[]{:S(2)}) async-start(), calls=%async_computation.3 | async-start | bytes 2228224
  407.7 439.2 %all-reduce.7.cloned.1.call-start = ((), (), s32[]{:S(2)}) async-start(), calls=%async_computation.6 | async-start | bytes 524288
  716.6 0.7 copy-start
  717.3 220.3 %reduce-scatter.9.cloned.1.call-start = ((), (), s32[]{:S(2)}) async-start(), calls=%async_computation.4 | async-start | bytes 2228224
Sparse Core Ops, SparseCore 0:
  281.6 122.4 all-reduce.4
  409.0 86.5 reduce-scatter.6
  717.5 129.4 all-reduce.6
  851.1 86.5 reduce-scatter.8
where the time goes:
time: 1100 us
  blocking collectives  579 us (53%)
  waiting for transfers between devices  426 us (39%)
  local copies, waits for them, and re-layouts  45.7 us (4%)
  other arithmetic  18.5 us (2%)
  between operations  17.3 us (2%)
    unnamed x8, waiting for transfers between devices  426 us
    psum x2, blocking collectives, per_device(): alpha_now = lax.psum(jnp.sum(vector * image_vec), ('ka', 'pb')) / entries  155 us
    psum x2, blocking collectives, per_device(): square = lax.psum(jnp.sum(residual * residual), ('ka', 'pb')) / entries  147 us
    psum x1, blocking collectives, per_device(): start_sum = lax.psum(jnp.sum(dipole * dipole), ('ka', 'pb'))  125 us
    all_gather x2, blocking collectives, per_device(): full_vector = lax.all_gather(cols_full, 'ka', axis=0, tiled=True)  49.8 us
    all_gather x2, blocking collectives, per_device(): lax.all_gather(vector.astype(jnp.bfloat16), 'pb', axis=1, tiled=True)  43.4 us
    all_gather x1, blocking collectives, per_device(): val_all = lax.all_gather(val_amp, 'pb', axis=0, tiled=True)  33.6 us
    all_gather x1, blocking collectives, per_device(): cond_all = lax.all_gather(cond_amp, 'ka', axis=0, tiled=True)  25.4 us
  transfers between devices with their start and end apart: 5, of which 4 were waited for; matrix products, arithmetic and copies ran while one was open for 0% of the time, Pallas kernels for 0%

commit v1 on v0

v1 whole, which is shorter than its diff:
```python
import functools
import math

import jax
import jax.numpy as jnp
from jax import lax
from jax.experimental import pallas as pl
from jax.experimental.pallas import tpu as pltpu
from jax.sharding import PartitionSpec as P

GX = 4
GY = 8
EPSILON = 1e-06
F32 = jnp.float32
BF16 = jnp.bfloat16
N = 16
VMEM_LIMIT = 48 * 1024 * 1024


def q_table(window, q_count):
    third_len = q_count // (GX * GY)
    coord_one = window // (GY * third_len)
    coord_two = window // third_len % GY
    coord_three = window % third_len
    shift_one = jnp.remainder(coord_one[:, None] - coord_one[None, :], GX)
    shift_two = jnp.remainder(coord_two[:, None] - coord_two[None, :], GY)
    shift_three = jnp.remainder(coord_three[:, None] - coord_three[None, :], third_len)
    return (shift_one * GY + shift_two) * third_len + shift_three


def pair_lists(window):
    chip = lax.axis_index("pb") // 2
    table = q_table(window, 128)
    local = table // 16 == chip
    column = jnp.arange(16, dtype=jnp.int32)
    code = table % 16 * 16 + column[None, :]
    before = jnp.sum(
        (local[:, None, :] & (column[None, None, :] < column[None, :, None])).astype(jnp.int32), axis=2
    )
    hit = local[:, None, :] & (before[:, None, :] == column[None, :, None])
    codes = jnp.sum(jnp.where(hit, code[:, None, :], 0), axis=2)
    counts = jnp.sum(local.astype(jnp.int32), axis=1)
    return codes, counts


def ring_peers(me):
    return [lax.rem(me + o, N) for o in range(1, N)]


def barrier_all(ka, pb):
    barrier = pltpu.get_barrier_semaphore()
    for peer in ring_peers(ka):
        pl.semaphore_signal(barrier, inc=1, device_id={"ka": peer}, device_id_type=pl.DeviceIdType.MESH)
    for peer in ring_peers(pb):
        pl.semaphore_signal(barrier, inc=1, device_id={"pb": peer}, device_id_type=pl.DeviceIdType.MESH)
    pl.semaphore_wait(barrier, 2 * (N - 1))


def send_all(axis, me, source, target, send_sem, recv_sem):
    copies = []
    for o, peer in enumerate(ring_peers(me)):
        copy = pltpu.make_async_remote_copy(
            src_ref=source(peer),
            dst_ref=target(me),
            send_sem=send_sem.at[o],
            recv_sem=recv_sem.at[me],
            device_id={axis: peer},
            device_id_type=pl.DeviceIdType.MESH,
        )
        copy.start()
        copies.append(copy)
    return copies


def recv_all(axis, me, target, send_sem, recv_sem):
    for o, peer in enumerate(ring_peers(me)):
        pltpu.make_async_remote_copy(
            src_ref=target(peer),
            dst_ref=target(peer),
            send_sem=send_sem.at[o],
            recv_sem=recv_sem.at[peer],
            device_id={axis: peer},
            device_id_type=pl.DeviceIdType.MESH,
        ).wait_recv()


def total(x):
    while x.ndim > 2:
        x = jnp.sum(x, axis=0)
    return jnp.sum(jnp.sum(x, axis=0, keepdims=True), axis=1, keepdims=True)


def stat_rows(values):
    row = lax.broadcasted_iota(jnp.int32, (16, 128), 0)
    block = jnp.zeros((16, 128), F32)
    for i, value in enumerate(values):
        rest = jnp.broadcast_to(value, (16, 128))
        for part in range(3):
            piece = rest.astype(BF16).astype(F32)
            block = jnp.where(row == 3 * i + part, piece, block)
            rest = rest - piece
    return block.astype(BF16)


def read_stat(block, i):
    return block[:, 3 * i : 3 * i + 1] + block[:, 3 * i + 1 : 3 * i + 2] + block[:, 3 * i + 2 : 3 * i + 3]


def gather_kernel(
    dip_ref, cond_ref, val_ref, w_ref,
    cond_out, val_out, w_out, row_out, dip_out,
    perm_ref, flat_ref, msg_ref,
    cond_s, cond_r, cpb_s, cpb_r, val_s, val_r, row_s, row_r, dip_s, dip_r, w_sem, own_sem,
):
    ka = lax.axis_index("ka")
    pb = lax.axis_index("pb")
    core = lax.rem(pb, 2)
    block = pb // 2
    to = lax.broadcasted_iota(jnp.int32, (64, 64), 0)
    fro = lax.broadcasted_iota(jnp.int32, (64, 64), 1)
    pick = (fro == 2 * lax.rem(to, 32) + to // 32).astype(F32).astype(BF16)
    perm_ref[...] = jnp.dot(pick, cond_ref[...], preferred_element_type=F32).astype(BF16)
    row_out[pb] = dip_ref[...]
    barrier_all(ka, pb)

    w_copy = pltpu.make_async_remote_copy(
        src_ref=w_ref.at[:, :, 1 - core],
        dst_ref=w_out.at[pl.ds(core * 8, 8)],
        send_sem=w_sem.at[0],
        recv_sem=w_sem.at[1],
        device_id={"pb": pb + 1 - 2 * core},
        device_id_type=pl.DeviceIdType.MESH,
    )
    row_c = send_all("pb", pb, lambda p: dip_ref, lambda p: row_out.at[p], row_s, row_r)
    cond_c = send_all("ka", ka, lambda p: perm_ref, lambda p: cond_out.at[block, p], cond_s, cond_r)
    w_copy.start()
    val_c = send_all("pb", pb, lambda p: val_ref, lambda p: val_out.at[p], val_s, val_r)
    own_cond = pltpu.make_async_copy(perm_ref, cond_out.at[block, ka], own_sem.at[0])
    own_cond.start()
    own_val = pltpu.make_async_copy(val_ref, val_out.at[pb], own_sem.at[1])
    own_val.start()
    own_w = pltpu.make_async_copy(w_ref.at[:, :, core], w_out.at[pl.ds(core * 8, 8)], own_sem.at[2])

    recv_all("pb", pb, lambda p: row_out.at[p], row_s, row_r)
    row = row_out[...]
    square = total(row * row)
    for i in range(N):
        flat_ref[2 * i : 2 * i + 2, :] = row_out[i]
    msg_ref[0:32, :] = flat_ref[...].astype(BF16)
    msg_ref[32:48, :] = stat_rows([square])
    dip_out[ka] = msg_ref[...]
    dip_c = send_all("ka", ka, lambda p: msg_ref, lambda p: dip_out.at[p], dip_s, dip_r)

    own_cond.wait()
    recv_all("ka", ka, lambda p: cond_out.at[block, p], cond_s, cond_r)
    cpb_c = []
    for o in range(1, 8):
        chip = lax.rem(block + o, 8)
        copy = pltpu.make_async_remote_copy(
            src_ref=cond_out.at[block],
            dst_ref=cond_out.at[block],
            send_sem=cpb_s.at[o],
            recv_sem=cpb_r.at[block],
            device_id={"pb": chip * 2 + core},
            device_id_type=pl.DeviceIdType.MESH,
        )
        copy.start()
        cpb_c.append(copy)
    own_w.start()
    recv_all("ka", ka, lambda p: dip_out.at[p], dip_s, dip_r)
    recv_all("pb", pb, lambda p: val_out.at[p], val_s, val_r)
    for o in range(1, 8):
        chip = lax.rem(block + o, 8)
        pltpu.make_async_remote_copy(
            src_ref=cond_out.at[chip],
            dst_ref=cond_out.at[chip],
            send_sem=cpb_s.at[o],
            recv_sem=cpb_r.at[chip],
            device_id={"pb": chip * 2 + core},
            device_id_type=pl.DeviceIdType.MESH,
        ).wait_recv()
    own_val.wait()
    own_w.wait()
    w_copy.wait_send()
    pltpu.make_async_remote_copy(
        src_ref=w_out.at[pl.ds((1 - core) * 8, 8)],
        dst_ref=w_out.at[pl.ds((1 - core) * 8, 8)],
        send_sem=w_sem.at[0],
        recv_sem=w_sem.at[1],
        device_id={"pb": pb + 1 - 2 * core},
        device_id_type=pl.DeviceIdType.MESH,
    ).wait_recv()
    for copy in row_c + cond_c + val_c + dip_c + cpb_c:
        copy.wait_send()


def gather(dipole, cond, val, w):
    sem = pltpu.SemaphoreType.DMA
    vmem = pl.BlockSpec(memory_space=pltpu.VMEM)
    anywhere = pl.BlockSpec(memory_space=pl.ANY)
    return pl.pallas_call(
        gather_kernel,
        out_shape=[
            jax.ShapeDtypeStruct((8, N, 64, 128), BF16),
            jax.ShapeDtypeStruct((N, 64, 128), BF16),
            jax.ShapeDtypeStruct((16, 8, 128, 128), BF16),
            jax.ShapeDtypeStruct((N, 2, 128), F32),
            jax.ShapeDtypeStruct((N, 48, 128), BF16),
        ],
        in_specs=[vmem, vmem, vmem, anywhere],
        out_specs=[anywhere, anywhere, anywhere, vmem, vmem],
        scratch_shapes=[
            pltpu.VMEM((64, 128), BF16),
            pltpu.VMEM((32, 128), F32),
            pltpu.VMEM((48, 128), BF16),
        ]
        + [sem((16,))] * 10
        + [sem((2,)), sem((3,))],
        compiler_params=pltpu.CompilerParams(
            collective_id=0, has_side_effects=True, vmem_limit_bytes=VMEM_LIMIT
        ),
        name="gather",
    )(dipole, cond, val, w)


def two_by_two(val):
    zero = jnp.zeros_like(val)
    return jnp.concatenate(
        [jnp.concatenate([val, zero], axis=1), jnp.concatenate([zero, val], axis=1)], axis=0
    )


def apply_kernel(codes, counts, u_ref, val_ref, cond_ref, w_ref, out_ref, half_ref, pair_ref, sum_ref):
    step = pl.program_id(0)

    @pl.when(step == 0)
    def _():
        sum_ref[...] = jnp.zeros_like(sum_ref)
        for k in range(N):
            both = jnp.dot(u_ref[k, 0:32, :], two_by_two(val_ref[k]), preferred_element_type=F32)
            half_ref[k, 0:32, :] = both[:, :128].astype(BF16)
            half_ref[k, 32:64, :] = both[:, 128:].astype(BF16)

    def cond_of(k):
        return jnp.concatenate([cond_ref[0, k], cond_ref[1, k]], axis=1)

    for k in range(N):
        pair_ref[k] = lax.dot_general(
            cond_of(k), half_ref[k], (((0,), (0,)), ((), ())), preferred_element_type=F32
        ).astype(BF16)

    for k in range(N):
        def add(n, acc):
            code = codes[k, n]
            q = code // 16
            other = code % 16
            w = w_ref[q].reshape(256, 128)
            return acc + (w * pair_ref[other]).astype(F32)

        acc = lax.fori_loop(0, counts[k], add, jnp.zeros((256, 128), F32))
        sum_ref[k] += jnp.dot(cond_of(k), acc.astype(BF16), preferred_element_type=F32)

    @pl.when(step == pl.num_programs(0) - 1)
    def _():
        for k in range(N):
            both = jnp.concatenate([sum_ref[k, 0:32, :], sum_ref[k, 32:64, :]], axis=1).astype(BF16)
            out_ref[k] = lax.dot_general(
                both, two_by_two(val_ref[k]), (((1,), (1,)), ((), ())), preferred_element_type=F32
            ).astype(BF16)


def apply(codes, counts, u, val, cond, w, name):
    grid_spec = pltpu.PrefetchScalarGridSpec(
        num_scalar_prefetch=2,
        grid=(4,),
        in_specs=[
            pl.BlockSpec(u.shape, lambda s, *_: (0, 0, 0)),
            pl.BlockSpec((N, 64, 128), lambda s, *_: (0, 0, 0)),
            pl.BlockSpec((2, N, 64, 128), lambda s, *_: (s, 0, 0, 0)),
            pl.BlockSpec((16, 2, 128, 128), lambda s, *_: (0, s, 0, 0)),
        ],
        out_specs=pl.BlockSpec((N, 32, 128), lambda s, *_: (0, 0, 0)),
        scratch_shapes=[
            pltpu.VMEM((N, 64, 128), BF16),
            pltpu.VMEM((N, 256, 128), BF16),
            pltpu.VMEM((N, 64, 128), F32),
        ],
    )
    return pl.pallas_call(
        apply_kernel,
        out_shape=jax.ShapeDtypeStruct((N, 32, 128), BF16),
        grid_spec=grid_spec,
        compiler_params=pltpu.CompilerParams(vmem_limit_bytes=VMEM_LIMIT),
        name=name,
    )(codes, counts, u, val, cond, w)


def reduce_scatter(ka, pb, part_ref, first_ref, cut_ref, second_ref, a_s, a_r, b_s, b_r):
    a_c = send_all("ka", ka, lambda p: part_ref.at[p], lambda p: first_ref.at[p], a_s, a_r)
    first_ref[ka] = part_ref[ka]
    recv_all("ka", ka, lambda p: first_ref.at[p], a_s, a_r)
    row = jnp.sum(first_ref[...].astype(F32), axis=0)
    for i in range(N):
        cut_ref[i] = row[2 * i : 2 * i + 2, :]
    b_c = send_all("pb", pb, lambda p: cut_ref.at[p], lambda p: second_ref.at[p], b_s, b_r)
    second_ref[pb] = cut_ref[pb]
    recv_all("pb", pb, lambda p: second_ref.at[p], b_s, b_r)
    return jnp.sum(second_ref[...], axis=0), a_c + b_c


def safe_divide(top, bottom):
    return jnp.where(bottom > 0, top / jnp.where(bottom > 0, bottom, 1.0), 0.0)


def middle_kernel(
    entries, factor,
    part_ref, dip_ref, energy_ref, row_ref, dips_ref,
    u_out, own_out, scalar_out,
    first_ref, cut_ref, second_ref, image_ref, mine_ref, flat_ref, msg_ref, all_ref,
    a_s, a_r, b_s, b_r, c_s, c_r, d_s, d_r,
):
    ka = lax.axis_index("ka")
    pb = lax.axis_index("pb")
    barrier_all(ka, pb)
    kernel_out, copies = reduce_scatter(
        ka, pb, part_ref, first_ref, cut_ref, second_ref, a_s, a_r, b_s, b_r
    )
    squares = read_stat(dips_ref[:, 32:48, :].astype(F32), 0)
    scale = 1.0 / jnp.sqrt(jnp.sum(squares, axis=0) / entries + EPSILON)
    own = dip_ref[...] * scale
    mine_ref[...] = energy_ref[...] * own - factor * scale * kernel_out
    image_ref[pb] = mine_ref[...]
    copies += send_all("pb", pb, lambda p: mine_ref, lambda p: image_ref.at[p], c_s, c_r)
    vector = row_ref[...] * scale
    norm = total(vector * vector)
    recv_all("pb", pb, lambda p: image_ref.at[p], c_s, c_r)
    image = image_ref[...]
    inner = total(vector * image)
    slope = safe_divide(inner, norm)
    rest = image - slope * vector
    left = total(rest * rest)
    for i in range(N):
        flat_ref[2 * i : 2 * i + 2, :] = rest[i]
    msg_ref[0:32, :] = flat_ref[...].astype(BF16)
    msg_ref[32:48, :] = stat_rows([inner, slope, left, norm])
    all_ref[ka] = msg_ref[...]
    copies += send_all("ka", ka, lambda p: msg_ref, lambda p: all_ref.at[p], d_s, d_r)
    recv_all("ka", ka, lambda p: all_ref.at[p], d_s, d_r)
    stats = all_ref[:, 32:48, :].astype(F32)
    slopes = read_stat(stats, 1)
    alpha = jnp.sum(read_stat(stats, 0), axis=0) / entries
    off = slopes - alpha
    square = jnp.sum(read_stat(stats, 2) + read_stat(stats, 3) * off * off, axis=0) / entries
    beta = jnp.sqrt(square + EPSILON)
    scaled = off * scale
    for k in range(N):
        u_out[k] = (
            all_ref[k, 0:32, :].astype(F32) + scaled[k] * dips_ref[k, 0:32, :].astype(F32)
        ).astype(BF16)
    own_out[0] = (mine_ref[...] - alpha * own) / beta
    own_out[1] = own
    scalar_out[...] = jnp.concatenate([alpha, beta], axis=0)
    for copy in copies:
        copy.wait_send()


def middle(entries, factor, part, dipole, energy, row, dips):
    sem = pltpu.SemaphoreType.DMA
    vmem = pl.BlockSpec(memory_space=pltpu.VMEM)
    return pl.pallas_call(
        functools.partial(middle_kernel, entries, factor),
        out_shape=[
            jax.ShapeDtypeStruct((N, 32, 128), BF16),
            jax.ShapeDtypeStruct((2, 2, 128), F32),
            jax.ShapeDtypeStruct((2, 128), F32),
        ],
        in_specs=[vmem] * 5,
        out_specs=[vmem] * 3,
        scratch_shapes=[
            pltpu.VMEM((N, 32, 128), BF16),
            pltpu.VMEM((N, 2, 128), F32),
            pltpu.VMEM((N, 2, 128), F32),
            pltpu.VMEM((N, 2, 128), F32),
            pltpu.VMEM((2, 128), F32),
            pltpu.VMEM((32, 128), F32),
            pltpu.VMEM((48, 128), BF16),
            pltpu.VMEM((N, 48, 128), BF16),
        ]
        + [sem((16,))] * 8,
        compiler_params=pltpu.CompilerParams(
            collective_id=1, has_side_effects=True, vmem_limit_bytes=VMEM_LIMIT
        ),
        name="middle",
    )(part, dipole, energy, row, dips)


def last_kernel(
    entries, factor,
    part_ref, energy_ref, own_ref, scalar_ref,
    u_out, coef_out,
    first_ref, cut_ref, second_ref, stat_ref, stats_ref, msg_ref, all_ref,
    a_s, a_r, b_s, b_r, c_s, c_r, d_s, d_r,
):
    ka = lax.axis_index("ka")
    pb = lax.axis_index("pb")
    barrier_all(ka, pb)
    kernel_out, copies = reduce_scatter(
        ka, pb, part_ref, first_ref, cut_ref, second_ref, a_s, a_r, b_s, b_r
    )
    alpha_zero = scalar_ref[0:1, :]
    beta_zero = scalar_ref[1:2, :]
    vector = own_ref[0]
    former = own_ref[1]
    image = energy_ref[...] * vector - factor / beta_zero * kernel_out
    rest = image - beta_zero * former
    norm = total(vector * vector)
    cross = total(vector * rest)
    slope = safe_divide(cross, norm)
    gap = rest - slope * vector
    row = lax.broadcasted_iota(jnp.int32, (8, 128), 0)

    def pack(values):
        block = jnp.zeros((8, 128), F32)
        for i, value in enumerate(values):
            block = jnp.where(row == i, jnp.broadcast_to(value, (8, 128)), block)
        return block

    stat_ref[...] = pack([total(vector * image), slope, total(gap * gap), norm])
    stats_ref[pb] = stat_ref[...]
    copies += send_all("pb", pb, lambda p: stat_ref, lambda p: stats_ref.at[p], c_s, c_r)
    recv_all("pb", pb, lambda p: stats_ref.at[p], c_s, c_r)

    def merge(block):
        inner, slopes, left, norms = [block[:, i : i + 1, :] for i in range(4)]
        norm = jnp.sum(norms, axis=0)
        slope = safe_divide(jnp.sum(norms * slopes, axis=0), norm)
        off = slopes - slope
        return jnp.sum(inner, axis=0), slope, jnp.sum(left + norms * off * off, axis=0), norm

    msg_ref[...] = pack(merge(stats_ref[...]))
    all_ref[ka] = msg_ref[...]
    copies += send_all("ka", ka, lambda p: msg_ref, lambda p: all_ref.at[p], d_s, d_r)
    recv_all("ka", ka, lambda p: all_ref.at[p], d_s, d_r)
    inner, slope, left, norm = merge(all_ref[...])
    alpha = inner / entries
    off = slope - alpha
    beta = jnp.sqrt((left + norm * off * off) / entries + EPSILON)
    u_out[...] = (rest - alpha * vector) / beta
    lane = lax.broadcasted_iota(jnp.int32, (1, 128), 1)
    coef_out[...] = jnp.where(
        lane == 0, alpha_zero, jnp.where(lane == 1, alpha, jnp.where(lane == 2, beta_zero, beta))
    )
    for copy in copies:
        copy.wait_send()


def last(entries, factor, part, energy, own, scalars):
    sem = pltpu.SemaphoreType.DMA
    vmem = pl.BlockSpec(memory_space=pltpu.VMEM)
    return pl.pallas_call(
        functools.partial(last_kernel, entries, factor),
        out_shape=[jax.ShapeDtypeStruct((2, 128), F32), jax.ShapeDtypeStruct((1, 128), F32)],
        in_specs=[vmem] * 4,
        out_specs=[vmem] * 2,
        scratch_shapes=[
            pltpu.VMEM((N, 32, 128), BF16),
            pltpu.VMEM((N, 2, 128), F32),
            pltpu.VMEM((N, 2, 128), F32),
            pltpu.VMEM((8, 128), F32),
            pltpu.VMEM((N, 8, 128), F32),
            pltpu.VMEM((8, 128), F32),
            pltpu.VMEM((N, 8, 128), F32),
        ]
        + [sem((16,))] * 8,
        compiler_params=pltpu.CompilerParams(
            collective_id=2, has_side_effects=True, vmem_limit_bytes=VMEM_LIMIT
        ),
        name="last",
    )(part, energy, own, scalars)


def per_device(dipole, energy, cond_amp, val_amp, screened, window):
    entries = 16 * 4096
    factor = 1.0 / (2048 * math.sqrt(entries))
    dipole = dipole.reshape(2, 128)
    energy = energy.reshape(2, 128)
    codes, counts = pair_lists(window)
    cond, val, w, row, dips = gather(
        dipole, cond_amp[0], val_amp[0], screened.reshape(8, 8, 2, 128, 128)
    )
    part = apply(codes, counts, dips, val, cond, w, "apply_first")
    vector, own, scalars = middle(entries, factor, part, dipole, energy, row, dips)
    part = apply(codes, counts, vector, val, cond, w, "apply_second")
    out, coef = last(entries, factor, part, energy, own, scalars)
    return coef[0, :4], out.reshape(1, 256)


def solution(mesh):
    in_specs = (
        P("ka", "pb"),
        P("ka", "pb"),
        P("ka", None, "pb"),
        P("pb", None, "ka"),
        P("pb", None, "ka"),
        P(),
    )
    out_specs = (P(), P("ka", "pb"))
    return jax.shard_map(
        per_device, mesh=mesh, in_specs=in_specs, out_specs=out_specs, check_vma=False
    )
```

time: 1100 us -> 191 us (0.17)
  blocking collectives: 579 us -> 0 us
  waiting for transfers between devices: 426 us -> 0 us
  Pallas kernels: 0 us -> 185 us
  local copies, waits for them, and re-layouts: 45.7 us -> 3.19 us
  other arithmetic: 18.5 us -> 1.58 us
  between operations: 17.3 us -> 0.73 us
    psum x5 -> x0, blocking collectives: 427 us -> none  [the longest x2 155 us: per_device(): alpha_now = lax.psum(jnp.sum(vector * image_vec), ('ka', 'pb')) / entries]
    unnamed x8 -> x0, waiting for transfers between devices: 426 us -> none
    pallas_call x0 -> x5, Pallas kernels: none -> 185 us  [the longest x1 84.8 us: gather(): pl.pallas_call(gather_kernel, out_shape=[jax.ShapeDtypeStruct((8, N, 64,...]
    all_gather x6 -> x0, blocking collectives: 152 us -> none  [the longest x2 49.8 us: per_device(): full_vector = lax.all_gather(cols_full, 'ka', axis=0, tiled=True)]
    gather x4 -> x0, local copies, waits for them, and re-layouts: 21 us -> none  [per_group(): picked = jnp.take(blocks, q_rows, axis=0)]
    unnamed x24 -> x9, local copies, waits for them, and re-layouts: 17.2 us -> 2.68 us
    dot_general x4 -> x0, other arithmetic: 12.3 us -> none  [per_group(): jnp.einsum('jkgh,kgh->jgh', picked, pair_dens, preferred_element_type=jnp...]
  transfers between devices with their start and end apart: 5 -> 0, of which waited for: 4 -> 0; matrix products, arithmetic and copies ran while one was open for 0% -> 0% of each run, Pallas kernels for 0% -> 0%
where the time goes in v1:
time: 191 us
  Pallas kernels  185 us (97%)
  local copies, waits for them, and re-layouts  3.19 us (2%)
    pallas_call x1, Pallas kernels, gather(): pl.pallas_call(gather_kernel, out_shape=[jax.ShapeDtypeStruct((8, N, 64,...  84.8 us
    pallas_call x2, Pallas kernels, apply(): pl.pallas_call(apply_kernel, out_shape=jax.ShapeDtypeStruct((N, 32, 128),...  42.3 us
    pallas_call x1, Pallas kernels, middle(): pl.pallas_call(functools.partial(middle_kernel, entries, factor), out_sha...  30.4 us
    pallas_call x1, Pallas kernels, last(): pl.pallas_call(functools.partial(last_kernel, entries, factor), out_shape...  27.7 us

profile of v1, /device:TPU:1, one launch (start us, length us, event | category | flops | bytes accessed | tf_op | source)
XLA Modules:
  0.0 190.6 jit_solution(14833305979104978253)
XLA Ops:
  0.6 0.7 and_select_fusion.3
  1.3 0.2 convert_reduce_fusion.1
  1.5 0.4 convert_reduce_fusion
  1.9 0.3 select_reduce_fusion.codes
  2.2 0.0 copy-start
  2.3 0.7 copy-done
  3.0 0.0 copy-start.1
  3.0 0.7 copy-done.1
  3.7 0.0 copy-start.2
  3.7 0.7 copy-done.2
  4.4 84.8 %gather.1 = (bf16[8,16,64,128]{3,2,1,0:T(8,128)(2,1)S(1)}, bf16[16,64,128]{2,1,0:T(8,128)(2,1)S(1)}, bf16[16,8,128,128]{3,2,1,0:T(8,128)(2,1)}, f32[16,2,128]{2,1,0:T(2,128)S(1)}, bf16[16,48,128]{2,1,0:T(8,128)(2,1)S(1)}) custom-call(f32[2,128]{1,0:T(2,128)S(1)} %bitcast.10, bf16[64,128]{1,0:T(8,128)(2,1)S(1)} %bitcast.8, bf16[64,128]{1,0:T(8,128)(2,1)S(1)} %bitcast.9, ...), custom_call_target="tpu_custom_call" | custom-call | tf_op jit(solution)/shard_map/gather/pallas_call | solution.py:201
  89.2 0.0 copy-start.3
  89.2 21.1 %apply_first.1.part_ref = bf16[16,32,128]{2,1,0:T(8,128)(2,1)S(1)} custom-call(s32[16,16]{1,0:T(8,128)S(1)} %select_reduce_fusion.codes, s32[16]{0:T(128)S(1)} %get-tuple-element.22.counts, bf16[16,48,128]{2,1,0:T(8,128)(2,1)S(1)} %get-tuple-element.12.u_ref.dips_ref, bf16[16,64,128]{2,1,0:T(8,128)(2,1)S(1)} %get-tuple-element.13.val_ref, ...), custom_call_target="tpu_custom_call" | custom-call | tf_op jit(solution)/shard_map/apply_first/pallas_call | solution.py:289
  110.3 0.0 copy-done.3
  110.4 30.4 %middle.1 = (bf16[16,32,128]{2,1,0:T(8,128)(2,1)S(1)}, f32[2,2,128]{2,1,0:T(2,128)S(1)}, f32[2,128]{1,0:T(2,128)S(1)}) custom-call(bf16[16,32,128]{2,1,0:T(8,128)(2,1)S(1)} %apply_first.1.part_ref, f32[2,128]{1,0:T(2,128)S(1)} %bitcast.11, f32[2,128]{1,0:T(2,128)S(1)} %bitcast.12, f32[16,2,128]{2,1,0:T(2,128)S(1)} %get-tuple-element.16.row_ref, ...), custom_call_target="tpu_custom_call" | custom-call | tf_op jit(solution)/shard_map/middle/pallas_call | solution.py:370
  140.7 21.1 %apply_second.1.part_ref = bf16[16,32,128]{2,1,0:T(8,128)(2,1)S(1)} custom-call(s32[16,16]{1,0:T(8,128)S(1)} %select_reduce_fusion.codes, s32[16]{0:T(128)S(1)} %get-tuple-element.22.counts, bf16[16,32,128]{2,1,0:T(8,128)(2,1)S(1)} %get-tuple-element.17.u_ref, bf16[16,64,128]{2,1,0:T(8,128)(2,1)S(1)} %get-tuple-element.13.val_ref, ...), custom_call_target="tpu_custom_call" | custom-call | tf_op jit(solution)/shard_map/apply_second/pallas_call | solution.py:289
  161.9 27.7 %last.1 = (f32[2,128]{1,0:T(2,128)S(1)}, f32[1,128]{1,0:T(1,128)S(1)}) custom-call(bf16[16,32,128]{2,1,0:T(8,128)(2,1)S(1)} %apply_second.1.part_ref, f32[2,128]{1,0:T(2,128)S(1)} %bitcast.13, f32[2,2,128]{2,1,0:T(2,128)S(1)} %get-tuple-element.18.own_ref, f32[2,128]{1,0:T(2,128)S(1)} %get-tuple-element.19.scalar_ref), custom_call_target="tpu_custom_call" | custom-call | tf_op jit(solution)/shard_map/last/pallas_call | solution.py:460
  189.6 0.5 slice_bitcast_fusion
  190.1 0.6 copy.9
  (1 shorter events, 0.0 us)
Async XLA Ops:
  2.2 0.7 copy-start
  3.0 0.7 copy-start.1
  3.7 0.7 copy-start.2
  89.2 21.2 %copy-start.3 = (f32[1,256]{1,0:T(1,128)S(1)}, f32[1,256]{1,0:T(1,128)}, u32[]{:S(2)}) copy-start(f32[1,256]{1,0:T(1,128)} %param.7) | copy-start | bytes 3076

commit v2 on v0

v2 whole, which is shorter than its diff:
```python
import functools
import math

import jax
import jax.numpy as jnp
from jax import lax
from jax.experimental import pallas as pl
from jax.experimental.pallas import tpu as pltpu
from jax.sharding import PartitionSpec as P

EPSILON = 1e-06
F32 = jnp.float32
BF16 = jnp.bfloat16
N = 16
NT = (((1,), (1,)), ((), ()))
MESH = pl.DeviceIdType.MESH


def ring_peers(me):
    return [lax.rem(me + o, N) for o in range(1, N)]


def signal_all(barrier, ka, pb):
    for peer in ring_peers(ka):
        pl.semaphore_signal(barrier, inc=1, device_id={"ka": peer}, device_id_type=MESH)
    for peer in ring_peers(pb):
        pl.semaphore_signal(barrier, inc=1, device_id={"pb": peer}, device_id_type=MESH)


def send_one(source, target, send_sem, recv_sem, device):
    copy = pltpu.make_async_remote_copy(
        src_ref=source,
        dst_ref=target,
        send_sem=send_sem,
        recv_sem=recv_sem,
        device_id=device,
        device_id_type=MESH,
    )
    copy.start()
    return copy


def recv_one(target, send_sem, recv_sem, device):
    pltpu.make_async_remote_copy(
        src_ref=target,
        dst_ref=target,
        send_sem=send_sem,
        recv_sem=recv_sem,
        device_id=device,
        device_id_type=MESH,
    ).wait_recv()


def send_all(axis, me, source, target, sems):
    return [
        send_one(source(peer), target(me), sems[0].at[o], sems[1].at[me], {axis: peer})
        for o, peer in enumerate(ring_peers(me))
    ]


def recv_all(axis, me, target, sems):
    for o, peer in enumerate(ring_peers(me)):
        recv_one(target(peer), sems[0].at[o], sems[1].at[peer], {axis: peer})


def total(x):
    while x.ndim > 2:
        x = jnp.sum(x, axis=0)
    return jnp.sum(jnp.sum(x, axis=0, keepdims=True), axis=1, keepdims=True)


def stat_rows(values):
    row = lax.broadcasted_iota(jnp.int32, (16, 128), 0)
    block = jnp.zeros((16, 128), F32)
    for i, value in enumerate(values):
        rest = jnp.broadcast_to(value, (16, 128))
        for part in range(3):
            piece = rest.astype(BF16).astype(F32)
            block = jnp.where(row == 3 * i + part, piece, block)
            rest = rest - piece
    return block.astype(BF16)


def read_stat(block, i):
    return block[:, 3 * i : 3 * i + 1] + block[:, 3 * i + 1 : 3 * i + 2] + block[:, 3 * i + 2 : 3 * i + 3]


def pack(values):
    row = lax.broadcasted_iota(jnp.int32, (8, 128), 0)
    block = jnp.zeros((8, 128), F32)
    for i, value in enumerate(values):
        block = jnp.where(row == i, jnp.broadcast_to(value, (8, 128)), block)
    return block


def safe_divide(top, bottom):
    return jnp.where(bottom > 0, top / jnp.where(bottom > 0, bottom, 1.0), 0.0)


def loop(count, body):
    def step(i, carry):
        body(i)
        return carry

    lax.fori_loop(0, count, step, 0)


def haydock_kernel(
    entries, factor,
    window_ref, dip_ref, energy_ref, cond_ref, val_ref, w_ref,
    u_out, coef_out,
    index_ref, perm_ref, cond_all, val_all, vv_ref, stage_ref, wt_ref,
    pack_ref, rows_ref, drow_ref, erow_ref, msg_ref, dips_ref, u_ref,
    half_ref, pair_ref, screen_ref, sum_ref, part_ref, first_ref, mine_ref, second_ref,
    after_ref, rests_ref, stat_ref, stats_ref, cut_ref,
    row_s, row_r, cond_s, cond_r, val_s, val_r, dip_s, dip_r, hop_s, hop_r, w_sem, own_sem,
    a_s, a_r, b_s, b_r, d_s, d_r, e_s, e_r,
):
    ka = lax.axis_index("ka")
    pb = lax.axis_index("pb")
    core = lax.rem(pb, 2)
    chip = pb // 2
    x = lax.rem(chip, 4)
    y = chip // 4
    across = (1 - y) * 4 + x
    barrier = pltpu.get_barrier_semaphore()
    signal_all(barrier, ka, pb)

    own_w = pltpu.make_async_copy(w_ref.at[:, :, core], stage_ref.at[pl.ds(core * 8, 8)], own_sem.at[0])
    own_w.start()
    to = lax.broadcasted_iota(jnp.int32, (64, 64), 0)
    fro = lax.broadcasted_iota(jnp.int32, (64, 64), 1)
    pick = (fro == 2 * lax.rem(to, 32) + to // 32).astype(F32).astype(BF16)
    perm_ref[...] = jnp.dot(pick, cond_ref[...], preferred_element_type=F32).astype(BF16)
    cond_all[chip, ka] = perm_ref[...]
    val_all[pb] = val_ref[...]
    pack_ref[0:2, :] = dip_ref[...]
    pack_ref[2:4, :] = energy_ref[...]
    rows_ref[pb] = pack_ref[...]
    pl.semaphore_wait(barrier, 2 * (N - 1))

    copies = send_all("ka", ka, lambda p: perm_ref, lambda p: cond_all.at[chip, p], (cond_s, cond_r))
    copies += send_all("pb", pb, lambda p: pack_ref, lambda p: rows_ref.at[p], (row_s, row_r))
    sibling = {"pb": pb + 1 - 2 * core}
    w_send = send_one(
        w_ref.at[:, :, 1 - core], stage_ref.at[pl.ds(core * 8, 8)], w_sem.at[0], w_sem.at[1], sibling
    )
    copies += [w_send]
    copies += send_all("pb", pb, lambda p: val_ref, lambda p: val_all.at[p], (val_s, val_r))

    def table(k):
        mine = window_ref[k]
        for other in range(N):
            theirs = window_ref[other]
            shift_one = jnp.bitwise_and(lax.shift_right_logical(mine, 5) - lax.shift_right_logical(theirs, 5), 3)
            shift_two = jnp.bitwise_and(lax.shift_right_logical(mine, 2) - lax.shift_right_logical(theirs, 2), 7)
            shift_three = jnp.bitwise_and(mine - theirs, 3)
            q = (shift_one * 8 + shift_two) * 4 + shift_three
            index_ref[k * N + other] = jnp.where(
                lax.shift_right_logical(q, 4) == chip, jnp.bitwise_and(q, 15), 16
            )

    loop(N, table)

    recv_all("pb", pb, lambda p: rows_ref.at[p], (row_s, row_r))
    for i in range(N):
        drow_ref[2 * i : 2 * i + 2, :] = rows_ref[i, 0:2, :]
        erow_ref[2 * i : 2 * i + 2, :] = rows_ref[i, 2:4, :]
    drow = drow_ref[...]
    msg_ref[0, 0:32, :] = drow.astype(BF16)
    msg_ref[0, 32:48, :] = stat_rows([total(drow * drow)])
    dips_ref[ka] = msg_ref[0]
    copies += send_all("ka", ka, lambda p: msg_ref.at[0], lambda p: dips_ref.at[p], (dip_s, dip_r))

    recv_all("ka", ka, lambda p: cond_all.at[chip, p], (cond_s, cond_r))
    lower = pl.ds(0, 8)
    upper = pl.ds(8, 8)
    x_chips = [y * 4 + lax.rem(x + o, 4) for o in range(1, 4)]

    def at(which):
        return {"pb": which * 2 + core}

    copies += [send_one(cond_all.at[chip], cond_all.at[chip], hop_s.at[0], hop_r.at[0], at(across))]
    for o in range(3):
        copies += [
            send_one(cond_all.at[chip], cond_all.at[chip], hop_s.at[1 + o], hop_r.at[1 + o], at(x_chips[o]))
        ]

    def turn(q):
        for j in range(8):
            wt_ref[j % 4, q, :, j // 4 * 128 : j // 4 * 128 + 128] = stage_ref[q, j].T

    own_w.wait()
    loop(8, lambda q: turn(core * 8 + q))
    for i in range(4):
        wt_ref[i, 16] = jnp.zeros((128, 256), BF16)
    recv_one(stage_ref.at[pl.ds((1 - core) * 8, 8)], w_sem.at[0], w_sem.at[1], sibling)
    loop(8, lambda q: turn((1 - core) * 8 + q))

    recv_all("pb", pb, lambda p: val_all.at[p], (val_s, val_r))

    def spread(k):
        turned = val_all[k].T
        zero = jnp.zeros_like(turned)
        vv_ref[k] = jnp.concatenate(
            [jnp.concatenate([turned, zero], axis=1), jnp.concatenate([zero, turned], axis=1)], axis=0
        )

    loop(N, spread)
    recv_all("ka", ka, lambda p: dips_ref.at[p], (dip_s, dip_r))

    def start_apply(vector_ref):
        def first(k):
            both = lax.dot_general(vv_ref[k], vector_ref[k, 0:32, :], NT, preferred_element_type=F32)
            half_ref[k, :, 0:32] = both[0:128].astype(BF16)
            half_ref[k, :, 32:64] = both[128:256].astype(BF16)
            sum_ref[k] = jnp.zeros((64, 128), F32)

        loop(N, first)

    def columns(part, k):
        return jnp.concatenate([cond_all[part, k], cond_all[part + 4, k]], axis=1)

    def apply_part(part):
        def pairs(k):
            pair_ref[k] = jnp.dot(half_ref[k], columns(part, k), preferred_element_type=F32).astype(BF16)

        def screen(k):
            for top in (0, 64):
                rows = slice(top, top + 64)
                acc = jnp.zeros((64, 256), F32)
                for other in range(0, N, 2):
                    one = wt_ref[part, index_ref[k * N + other], rows, :] * pair_ref[other, rows, :]
                    two = wt_ref[part, index_ref[k * N + other + 1], rows, :] * pair_ref[other + 1, rows, :]
                    acc = acc + (one + two).astype(F32)
                screen_ref[rows, :] = acc.astype(BF16)
            sum_ref[k] += lax.dot_general(columns(part, k), screen_ref[...], NT, preferred_element_type=F32)

        loop(N, pairs)
        loop(N, screen)

    def finish_apply(which):
        def one(k):
            both = jnp.concatenate([sum_ref[k, 0:32, :], sum_ref[k, 32:64, :]], axis=1)
            high = both.astype(BF16)
            low = (both - high.astype(F32)).astype(BF16)
            part_ref[which, k] = (
                jnp.dot(high, vv_ref[k], preferred_element_type=F32)
                + jnp.dot(low, vv_ref[k], preferred_element_type=F32)
            ).astype(BF16)

        loop(N, one)

    start_apply(dips_ref)
    recv_one(cond_all.at[across], hop_s.at[0], hop_r.at[0], at(across))
    for o in range(3):
        copies.append(
            send_one(
                cond_all.at[across, lower], cond_all.at[across, lower], hop_s.at[4 + o], hop_r.at[4 + o], at(x_chips[o])
            )
        )
    apply_part(x)
    for o in (0, 2, 1):
        back = x_chips[2 - o]
        recv_one(cond_all.at[back], hop_s.at[1 + o], hop_r.at[1 + o], at(back))
        copies.append(
            send_one(
                cond_all.at[back, upper], cond_all.at[back, upper], hop_s.at[7 + o], hop_r.at[7 + o], at(across)
            )
        )
    for o in (0, 2, 1):
        back = x_chips[2 - o]
        far = (1 - y) * 4 + lax.rem(back, 4)
        recv_one(cond_all.at[far, lower], hop_s.at[4 + o], hop_r.at[4 + o], at(back))
        recv_one(cond_all.at[far, upper], hop_s.at[7 + o], hop_r.at[7 + o], at(across))
        apply_part(lax.rem(back, 4))
    finish_apply(0)

    def reduce_rows(which):
        new = send_all(
            "ka", ka, lambda p: part_ref.at[which, p], lambda p: first_ref.at[which, p], (a_s.at[which], a_r.at[which])
        )
        first_ref[which, ka] = part_ref[which, ka]
        recv_all("ka", ka, lambda p: first_ref.at[which, p], (a_s.at[which], a_r.at[which]))
        mine_ref[which] = jnp.sum(first_ref[which].astype(F32), axis=0).astype(BF16)
        second_ref[which, pb] = mine_ref[which]
        new += send_all(
            "pb", pb, lambda p: mine_ref.at[which], lambda p: second_ref.at[which, p], (b_s.at[which], b_r.at[which])
        )
        recv_all("pb", pb, lambda p: second_ref.at[which, p], (b_s.at[which], b_r.at[which]))
        return jnp.sum(second_ref[which].astype(F32), axis=0), new

    kernel_row, new = reduce_rows(0)
    copies += new
    squares = read_stat(dips_ref[:, 32:48, :].astype(F32), 0)
    scale = 1.0 / jnp.sqrt(jnp.sum(squares, axis=0) / entries + EPSILON)
    vector = drow_ref[...] * scale
    image = erow_ref[...] * vector - factor * scale * kernel_row
    norm = total(vector * vector)
    inner = total(vector * image)
    slope = safe_divide(inner, norm)
    rest = image - slope * vector
    msg_ref[1, 0:32, :] = rest.astype(BF16)
    msg_ref[1, 32:48, :] = stat_rows([inner, slope, total(rest * rest), norm])
    rests_ref[ka] = msg_ref[1]
    copies += send_all("ka", ka, lambda p: msg_ref.at[1], lambda p: rests_ref.at[p], (d_s, d_r))
    recv_all("ka", ka, lambda p: rests_ref.at[p], (d_s, d_r))
    stats = rests_ref[:, 32:48, :].astype(F32)
    alpha_zero = jnp.sum(read_stat(stats, 0), axis=0) / entries
    off = read_stat(stats, 1) - alpha_zero
    square = jnp.sum(read_stat(stats, 2) + read_stat(stats, 3) * off * off, axis=0) / entries
    beta_zero = jnp.sqrt(square + EPSILON)
    scaled = off * scale
    for k in range(N):
        u_ref[k] = (
            rests_ref[k, 0:32, :].astype(F32) + scaled[k] * dips_ref[k, 0:32, :].astype(F32)
        ).astype(BF16)
    after_ref[0] = vector
    after_ref[1] = (image - alpha_zero * vector) / beta_zero

    start_apply(u_ref)
    loop(4, apply_part)
    finish_apply(1)
    kernel_row, new = reduce_rows(1)
    copies += new
    former = after_ref[0]
    vector = after_ref[1]
    image = erow_ref[...] * vector - factor / beta_zero * kernel_row
    rest = image - beta_zero * former
    norm = total(vector * vector)
    slope = safe_divide(total(vector * rest), norm)
    gap = rest - slope * vector
    stat_ref[...] = pack([total(vector * image), slope, total(gap * gap), norm])
    stats_ref[ka] = stat_ref[...]
    copies += send_all("ka", ka, lambda p: stat_ref, lambda p: stats_ref.at[p], (e_s, e_r))
    recv_all("ka", ka, lambda p: stats_ref.at[p], (e_s, e_r))
    inners, slopes, lefts, norms = [stats_ref[:, i : i + 1, :] for i in range(4)]
    alpha = jnp.sum(inners, axis=0) / entries
    off = slopes - alpha
    beta = jnp.sqrt(jnp.sum(lefts + norms * off * off, axis=0) / entries + EPSILON)
    last = (rest - alpha * vector) / beta
    for i in range(N):
        cut_ref[i] = last[2 * i : 2 * i + 2, :]
    u_out[...] = cut_ref[pb]
    lane = lax.broadcasted_iota(jnp.int32, (1, 128), 1)
    coef_out[...] = jnp.where(
        lane == 0, alpha_zero, jnp.where(lane == 1, alpha, jnp.where(lane == 2, beta_zero, beta))
    )
    for copy in copies:
        copy.wait_send()


def haydock(entries, factor, *args):
    sem = pltpu.SemaphoreType.DMA
    vmem = pl.BlockSpec(memory_space=pltpu.VMEM)
    pair = [sem((N,)), sem((N,))]
    return pl.pallas_call(
        functools.partial(haydock_kernel, entries, factor),
        out_shape=[jax.ShapeDtypeStruct((2, 128), F32), jax.ShapeDtypeStruct((1, 128), F32)],
        in_specs=[pl.BlockSpec(memory_space=pltpu.SMEM)] + [vmem] * 4 + [pl.BlockSpec(memory_space=pl.ANY)],
        out_specs=[vmem] * 2,
        scratch_shapes=[
            pltpu.SMEM((N * N,), jnp.int32),
            pltpu.VMEM((64, 128), BF16),
            pltpu.VMEM((8, N, 64, 128), BF16),
            pltpu.VMEM((N, 64, 128), BF16),
            pltpu.VMEM((N, 256, 128), BF16),
            pltpu.VMEM((16, 8, 128, 128), BF16),
            pltpu.VMEM((4, 17, 128, 256), BF16),
            pltpu.VMEM((4, 128), F32),
            pltpu.VMEM((N, 4, 128), F32),
            pltpu.VMEM((32, 128), F32),
            pltpu.VMEM((32, 128), F32),
            pltpu.VMEM((2, 48, 128), BF16),
            pltpu.VMEM((N, 48, 128), BF16),
            pltpu.VMEM((N, 32, 128), BF16),
            pltpu.VMEM((N, 128, 64), BF16),
            pltpu.VMEM((N, 128, 256), BF16),
            pltpu.VMEM((128, 256), BF16),
            pltpu.VMEM((N, 64, 128), F32),
            pltpu.VMEM((2, N, 32, 128), BF16),
            pltpu.VMEM((2, N, 32, 128), BF16),
            pltpu.VMEM((2, 32, 128), BF16),
            pltpu.VMEM((2, N, 32, 128), BF16),
            pltpu.VMEM((2, 32, 128), F32),
            pltpu.VMEM((N, 48, 128), BF16),
            pltpu.VMEM((8, 128), F32),
            pltpu.VMEM((N, 8, 128), F32),
            pltpu.VMEM((N, 2, 128), F32),
        ]
        + pair * 5
        + [sem((2,)), sem((1,))]
        + [sem((2, N))] * 4
        + pair * 2,
        compiler_params=pltpu.CompilerParams(
            collective_id=0, has_side_effects=True, vmem_limit_bytes=48 * 1024 * 1024
        ),
        name="haydock",
    )(*args)


def per_device(dipole, energy, cond_amp, val_amp, screened, window):
    entries = 16 * 4096
    factor = 1.0 / (2048 * math.sqrt(entries))
    out, coef = haydock(
        entries,
        factor,
        window,
        dipole.reshape(2, 128),
        energy.reshape(2, 128),
        cond_amp[0],
        val_amp[0],
        screened.reshape(8, 8, 2, 128, 128),
    )
    return coef[0, :4], out.reshape(1, 256)


def solution(mesh):
    in_specs = (
        P("ka", "pb"),
        P("ka", "pb"),
        P("ka", None, "pb"),
        P("pb", None, "ka"),
        P("pb", None, "ka"),
        P(),
    )
    out_specs = (P(), P("ka", "pb"))
    return jax.shard_map(
        per_device, mesh=mesh, in_specs=in_specs, out_specs=out_specs, check_vma=False
    )
```

time: 1100 us -> 142 us (0.13)
  blocking collectives: 579 us -> 0 us
  waiting for transfers between devices: 426 us -> 0 us
  Pallas kernels: 0 us -> 135 us
  local copies, waits for them, and re-layouts: 45.7 us -> 6.7 us
  other arithmetic: 18.5 us -> 0 us
  between operations: 17.3 us -> 0.65 us
    psum x5 -> x0, blocking collectives: 427 us -> none  [the longest x2 155 us: per_device(): alpha_now = lax.psum(jnp.sum(vector * image_vec), ('ka', 'pb')) / entries]
    unnamed x8 -> x0, waiting for transfers between devices: 426 us -> none
    all_gather x6 -> x0, blocking collectives: 152 us -> none  [the longest x2 49.8 us: per_device(): full_vector = lax.all_gather(cols_full, 'ka', axis=0, tiled=True)]
    pallas_call x0 -> x1, Pallas kernels: none -> 135 us  [haydock(): pl.pallas_call(functools.partial(haydock_kernel, entries, factor), out_sh...]
    gather x4 -> x0, local copies, waits for them, and re-layouts: 21 us -> none  [per_group(): picked = jnp.take(blocks, q_rows, axis=0)]
    dot_general x4 -> x0, other arithmetic: 12.3 us -> none  [per_group(): jnp.einsum('jkgh,kgh->jgh', picked, pair_dens, preferred_element_type=jnp...]
    unnamed x24 -> x13, local copies, waits for them, and re-layouts: 17.2 us -> 6.19 us
  transfers between devices with their start and end apart: 5 -> 0, of which waited for: 4 -> 0; matrix products, arithmetic and copies ran while one was open for 0% -> 0% of each run, Pallas kernels for 0% -> 0%
where the time goes in v2:
time: 142 us
  Pallas kernels  135 us (95%)
  local copies, waits for them, and re-layouts  6.7 us (5%)
    pallas_call x1, Pallas kernels, haydock(): pl.pallas_call(functools.partial(haydock_kernel, entries, factor), out_sh...  135 us
    unnamed x13, local copies, waits for them, and re-layouts  6.19 us

profile of v2, /device:TPU:1, one launch (start us, length us, event | category | flops | bytes accessed | tf_op | source)
XLA Modules:
  0.0 142.2 jit_solution(17098169979464081360)
XLA Ops:
  0.6 0.0 copy-start
  0.6 2.2 %copy-done = bf16[8,2048,128]{2,1,0:T(8,128)(2,1)S(1)} copy-done((bf16[8,2048,128]{2,1,0:T(8,128)(2,1)S(1)}, bf16[8,2048,128]{2,1,0:T(8,128)(2,1)}, u32[]{:S(2)}) %copy-start) | copy-done | bytes 4194328
  2.8 0.0 copy-start.1
  2.8 0.7 copy-done.1
  3.5 0.0 copy-start.2
  3.5 0.7 copy-done.2
  4.3 0.0 copy-start.3
  4.3 0.7 copy-done.3
  4.9 0.0 copy-start.4
  4.9 0.7 copy-done.4
  5.6 0.0 copy-start.5
  5.6 0.7 copy-done.5
  6.3 134.8 %haydock.1 = (f32[2,128]{1,0:T(2,128)S(1)}, f32[1,128]{1,0:T(1,128)S(1)}) custom-call(s32[16]{0:T(128)S(1)} %copy-done.5, f32[2,128]{1,0:T(2,128)S(1)} %bitcast.12, f32[2,128]{1,0:T(2,128)S(1)} %bitcast.13, bf16[64,128]{1,0:T(8,128)(2,1)S(1)} %bitcast.9, bf16[64,128]{1,0:T(8,128)(2,1)S(1)} %bitcast.10, bf16[8,8,2,128,128]{4,3,2,1,0:T(8,128)(2,1)S(1)} %bitcast.8), custom_call_target="tpu_custom_call" | custom-call | tf_op jit(solution)/shard_map/haydock/pallas_call | solution.py:357
  141.1 0.5 slice_bitcast_fusion
  141.6 0.6 copy.9
Async XLA Ops:
  0.6 2.2 %copy-start = (bf16[8,2048,128]{2,1,0:T(8,128)(2,1)S(1)}, bf16[8,2048,128]{2,1,0:T(8,128)(2,1)}, u32[]{:S(2)}) copy-start(bf16[8,2048,128]{2,1,0:T(8,128)(2,1)} %param.10) | copy-start | bytes 12582916
  2.8 0.7 copy-start.1
  3.5 0.7 copy-start.2
  4.3 0.7 copy-start.3
  4.9 0.7 copy-start.4
  5.6 0.7 copy-start.5

commit v3 on v2

--- a/solution.py
+++ b/solution.py
@@ -109,7 +109,7 @@
     entries, factor,
     window_ref, dip_ref, energy_ref, cond_ref, val_ref, w_ref,
     u_out, coef_out,
-    index_ref, perm_ref, cond_all, val_all, vv_ref, stage_ref, wt_ref,
+    grid_ref, index_ref, perm_ref, cond_all, val_all, vv_ref, stage_ref, wt_ref,
     pack_ref, rows_ref, drow_ref, erow_ref, msg_ref, dips_ref, u_ref,
     half_ref, pair_ref, screen_ref, sum_ref, part_ref, first_ref, mine_ref, second_ref,
     after_ref, rests_ref, stat_ref, stats_ref, cut_ref,
@@ -126,32 +126,45 @@
     barrier = pltpu.get_barrier_semaphore()
     signal_all(barrier, ka, pb)
 
+    loads = [
+        pltpu.make_async_copy(source, target, own_sem.at[1 + i])
+        for i, (source, target) in enumerate(
+            [
+                (cond_ref, perm_ref.at[0]),
+                (dip_ref, pack_ref.at[0]),
+                (energy_ref, pack_ref.at[1]),
+                (val_ref, val_all.at[pb]),
+                (window_ref, grid_ref),
+            ]
+        )
+    ]
+    for load in loads:
+        load.start()
     own_w = pltpu.make_async_copy(w_ref.at[:, :, core], stage_ref.at[pl.ds(core * 8, 8)], own_sem.at[0])
     own_w.start()
     to = lax.broadcasted_iota(jnp.int32, (64, 64), 0)
     fro = lax.broadcasted_iota(jnp.int32, (64, 64), 1)
     pick = (fro == 2 * lax.rem(to, 32) + to // 32).astype(F32).astype(BF16)
-    perm_ref[...] = jnp.dot(pick, cond_ref[...], preferred_element_type=F32).astype(BF16)
-    cond_all[chip, ka] = perm_ref[...]
-    val_all[pb] = val_ref[...]
-    pack_ref[0:2, :] = dip_ref[...]
-    pack_ref[2:4, :] = energy_ref[...]
+    for load in loads:
+        load.wait()
+    perm_ref[1] = jnp.dot(pick, perm_ref[0], preferred_element_type=F32).astype(BF16)
+    cond_all[chip, ka] = perm_ref[1]
     rows_ref[pb] = pack_ref[...]
     pl.semaphore_wait(barrier, 2 * (N - 1))
 
-    copies = send_all("ka", ka, lambda p: perm_ref, lambda p: cond_all.at[chip, p], (cond_s, cond_r))
+    copies = send_all("ka", ka, lambda p: perm_ref.at[1], lambda p: cond_all.at[chip, p], (cond_s, cond_r))
     copies += send_all("pb", pb, lambda p: pack_ref, lambda p: rows_ref.at[p], (row_s, row_r))
     sibling = {"pb": pb + 1 - 2 * core}
     w_send = send_one(
         w_ref.at[:, :, 1 - core], stage_ref.at[pl.ds(core * 8, 8)], w_sem.at[0], w_sem.at[1], sibling
     )
     copies += [w_send]
-    copies += send_all("pb", pb, lambda p: val_ref, lambda p: val_all.at[p], (val_s, val_r))
+    copies += send_all("pb", pb, lambda p: val_all.at[pb], lambda p: val_all.at[p], (val_s, val_r))
 
     def table(k):
-        mine = window_ref[k]
+        mine = grid_ref[k]
         for other in range(N):
-            theirs = window_ref[other]
+            theirs = grid_ref[other]
             shift_one = jnp.bitwise_and(lax.shift_right_logical(mine, 5) - lax.shift_right_logical(theirs, 5), 3)
             shift_two = jnp.bitwise_and(lax.shift_right_logical(mine, 2) - lax.shift_right_logical(theirs, 2), 7)
             shift_three = jnp.bitwise_and(mine - theirs, 3)
@@ -164,8 +177,8 @@
 
     recv_all("pb", pb, lambda p: rows_ref.at[p], (row_s, row_r))
     for i in range(N):
-        drow_ref[2 * i : 2 * i + 2, :] = rows_ref[i, 0:2, :]
-        erow_ref[2 * i : 2 * i + 2, :] = rows_ref[i, 2:4, :]
+        drow_ref[2 * i : 2 * i + 2, :] = rows_ref[i, 0]
+        erow_ref[2 * i : 2 * i + 2, :] = rows_ref[i, 1]
     drow = drow_ref[...]
     msg_ref[0, 0:32, :] = drow.astype(BF16)
     msg_ref[0, 32:48, :] = stat_rows([total(drow * drow)])
@@ -210,37 +223,30 @@
     recv_all("ka", ka, lambda p: dips_ref.at[p], (dip_s, dip_r))
 
     def start_apply(vector_ref):
-        def first(k):
+        for k in range(N):
             both = lax.dot_general(vv_ref[k], vector_ref[k, 0:32, :], NT, preferred_element_type=F32)
             half_ref[k, :, 0:32] = both[0:128].astype(BF16)
             half_ref[k, :, 32:64] = both[128:256].astype(BF16)
             sum_ref[k] = jnp.zeros((64, 128), F32)
 
-        loop(N, first)
-
     def columns(part, k):
         return jnp.concatenate([cond_all[part, k], cond_all[part + 4, k]], axis=1)
 
     def apply_part(part):
-        def pairs(k):
+        def screen(k):
+            acc = jnp.zeros((128, 256), BF16)
+            for other in range(N):
+                acc = acc + wt_ref[part, index_ref[k * N + other]] * pair_ref[other]
+            screen_ref[k] = acc
+
+        for k in range(N):
             pair_ref[k] = jnp.dot(half_ref[k], columns(part, k), preferred_element_type=F32).astype(BF16)
-
-        def screen(k):
-            for top in (0, 64):
-                rows = slice(top, top + 64)
-                acc = jnp.zeros((64, 256), F32)
-                for other in range(0, N, 2):
-                    one = wt_ref[part, index_ref[k * N + other], rows, :] * pair_ref[other, rows, :]
-                    two = wt_ref[part, index_ref[k * N + other + 1], rows, :] * pair_ref[other + 1, rows, :]
-                    acc = acc + (one + two).astype(F32)
-                screen_ref[rows, :] = acc.astype(BF16)
-            sum_ref[k] += lax.dot_general(columns(part, k), screen_ref[...], NT, preferred_element_type=F32)
-
-        loop(N, pairs)
         loop(N, screen)
+        for k in range(N):
+            sum_ref[k] += lax.dot_general(columns(part, k), screen_ref[k], NT, preferred_element_type=F32)
 
     def finish_apply(which):
-        def one(k):
+        for k in range(N):
             both = jnp.concatenate([sum_ref[k, 0:32, :], sum_ref[k, 32:64, :]], axis=1)
             high = both.astype(BF16)
             low = (both - high.astype(F32)).astype(BF16)
@@ -248,8 +254,6 @@
                 jnp.dot(high, vv_ref[k], preferred_element_type=F32)
                 + jnp.dot(low, vv_ref[k], preferred_element_type=F32)
             ).astype(BF16)
-
-        loop(N, one)
 
     start_apply(dips_ref)
     recv_one(cond_all.at[across], hop_s.at[0], hop_r.at[0], at(across))
@@ -357,18 +361,19 @@
     return pl.pallas_call(
         functools.partial(haydock_kernel, entries, factor),
         out_shape=[jax.ShapeDtypeStruct((2, 128), F32), jax.ShapeDtypeStruct((1, 128), F32)],
-        in_specs=[pl.BlockSpec(memory_space=pltpu.SMEM)] + [vmem] * 4 + [pl.BlockSpec(memory_space=pl.ANY)],
+        in_specs=[pl.BlockSpec(memory_space=pl.ANY)] * 6,
         out_specs=[vmem] * 2,
         scratch_shapes=[
+            pltpu.SMEM((N,), jnp.int32),
             pltpu.SMEM((N * N,), jnp.int32),
-            pltpu.VMEM((64, 128), BF16),
+            pltpu.VMEM((2, 64, 128), BF16),
             pltpu.VMEM((8, N, 64, 128), BF16),
             pltpu.VMEM((N, 64, 128), BF16),
             pltpu.VMEM((N, 256, 128), BF16),
             pltpu.VMEM((16, 8, 128, 128), BF16),
             pltpu.VMEM((4, 17, 128, 256), BF16),
-            pltpu.VMEM((4, 128), F32),
-            pltpu.VMEM((N, 4, 128), F32),
+            pltpu.VMEM((2, 2, 128), F32),
+            pltpu.VMEM((N, 2, 2, 128), F32),
             pltpu.VMEM((32, 128), F32),
             pltpu.VMEM((32, 128), F32),
             pltpu.VMEM((2, 48, 128), BF16),
@@ -376,7 +381,7 @@
             pltpu.VMEM((N, 32, 128), BF16),
             pltpu.VMEM((N, 128, 64), BF16),
             pltpu.VMEM((N, 128, 256), BF16),
-            pltpu.VMEM((128, 256), BF16),
+            pltpu.VMEM((N, 128, 256), BF16),
             pltpu.VMEM((N, 64, 128), F32),
             pltpu.VMEM((2, N, 32, 128), BF16),
             pltpu.VMEM((2, N, 32, 128), BF16),
@@ -389,7 +394,7 @@
             pltpu.VMEM((N, 2, 128), F32),
         ]
         + pair * 5
-        + [sem((2,)), sem((1,))]
+        + [sem((2,)), sem((6,))]
         + [sem((2, N))] * 4
         + pair * 2,
         compiler_params=pltpu.CompilerParams(

time: 142 us -> 105 us (0.74)
  Pallas kernels: 135 us -> 97 us
    pallas_call x1, Pallas kernels: 135 us -> 97 us  [haydock(): pl.pallas_call(functools.partial(haydock_kernel, entries, factor), out_sh...]
where the time goes in v3:
time: 105 us; the launch traced here: 104 us
  Pallas kernels  97 us (92%)
  local copies, waits for them, and re-layouts  6.7 us (6%)
    pallas_call x1, Pallas kernels, haydock(): pl.pallas_call(functools.partial(haydock_kernel, entries, factor), out_sh...  97 us
    unnamed x13, local copies, waits for them, and re-layouts  6.19 us

profile of v3, /device:TPU:1, one launch (start us, length us, event | category | flops | bytes accessed | tf_op | source)
XLA Modules:
  0.0 104.4 jit_solution(7510512659127142051)
XLA Ops:
  0.6 0.0 copy-start
  0.6 2.2 %copy-done = bf16[8,2048,128]{2,1,0:T(8,128)(2,1)S(1)} copy-done((bf16[8,2048,128]{2,1,0:T(8,128)(2,1)S(1)}, bf16[8,2048,128]{2,1,0:T(8,128)(2,1)}, u32[]{:S(2)}) %copy-start) | copy-done | bytes 4194328
  2.8 0.0 copy-start.1
  2.8 0.7 copy-done.1
  3.5 0.0 copy-start.2
  3.5 0.7 copy-done.2
  4.3 0.0 copy-start.3
  4.3 0.7 copy-done.3
  4.9 0.0 copy-start.4
  4.9 0.7 copy-done.4
  5.6 0.0 copy-start.5
  5.6 0.7 copy-done.5
  6.3 97.0 %haydock.1 = (f32[2,128]{1,0:T(2,128)S(1)}, f32[1,128]{1,0:T(1,128)S(1)}) custom-call(s32[16]{0:T(128)S(1)} %copy-done.5, f32[2,128]{1,0:T(2,128)S(1)} %bitcast.12, f32[2,128]{1,0:T(2,128)S(1)} %bitcast.13, bf16[64,128]{1,0:T(8,128)(2,1)S(1)} %bitcast.9, bf16[64,128]{1,0:T(8,128)(2,1)S(1)} %bitcast.10, bf16[8,8,2,128,128]{4,3,2,1,0:T(8,128)(2,1)S(1)} %bitcast.8), custom_call_target="tpu_custom_call" | custom-call | tf_op jit(solution)/shard_map/haydock/pallas_call | solution.py:361
  103.3 0.5 slice_bitcast_fusion
  103.8 0.6 copy.9
Async XLA Ops:
  0.6 2.2 %copy-start = (bf16[8,2048,128]{2,1,0:T(8,128)(2,1)S(1)}, bf16[8,2048,128]{2,1,0:T(8,128)(2,1)}, u32[]{:S(2)}) copy-start(bf16[8,2048,128]{2,1,0:T(8,128)(2,1)} %param.10) | copy-start | bytes 12582916
  2.8 0.7 copy-start.1
  3.5 0.7 copy-start.2
  4.3 0.7 copy-start.3
  4.9 0.7 copy-start.4
  5.6 0.7 copy-start.5

commit v4 on v3

--- a/solution.py
+++ b/solution.py
@@ -108,12 +108,12 @@
 def haydock_kernel(
     entries, factor,
     window_ref, dip_ref, energy_ref, cond_ref, val_ref, w_ref,
-    u_out, coef_out,
+    out_ref,
     grid_ref, index_ref, perm_ref, cond_all, val_all, vv_ref, stage_ref, wt_ref,
     pack_ref, rows_ref, drow_ref, erow_ref, msg_ref, dips_ref, u_ref,
     half_ref, pair_ref, screen_ref, sum_ref, part_ref, first_ref, mine_ref, second_ref,
     after_ref, rests_ref, stat_ref, stats_ref, cut_ref,
-    row_s, row_r, cond_s, cond_r, val_s, val_r, dip_s, dip_r, hop_s, hop_r, w_sem, own_sem,
+    row_s, row_r, few_s, few_r, far_s, far_r, cond_s, cond_r, val_s, val_r, dip_s, dip_r, hop_s, hop_r, w_sem, own_sem,
     a_s, a_r, b_s, b_r, d_s, d_r, e_s, e_r,
 ):
     ka = lax.axis_index("ka")
@@ -122,7 +122,6 @@
     chip = pb // 2
     x = lax.rem(chip, 4)
     y = chip // 4
-    across = (1 - y) * 4 + x
     barrier = pltpu.get_barrier_semaphore()
     signal_all(barrier, ka, pb)
 
@@ -148,11 +147,24 @@
     for load in loads:
         load.wait()
     perm_ref[1] = jnp.dot(pick, perm_ref[0], preferred_element_type=F32).astype(BF16)
-    cond_all[chip, ka] = perm_ref[1]
+    cond_all[y, x, ka] = perm_ref[1]
     rows_ref[pb] = pack_ref[...]
     pl.semaphore_wait(barrier, 2 * (N - 1))
 
-    copies = send_all("ka", ka, lambda p: perm_ref.at[1], lambda p: cond_all.at[chip, p], (cond_s, cond_r))
+    most = pl.ds(0, 48)
+    few = pl.ds(48, 16)
+    chips = [lax.rem(chip + o, 8) for o in range(1, 8)]
+
+    def at(which):
+        return {"pb": which * 2 + core}
+
+    copies = [
+        send_one(perm_ref.at[1, few], cond_all.at[y, x, ka, few], few_s.at[o], few_r.at[chip], at(other))
+        for o, other in enumerate(chips)
+    ]
+    copies += send_all(
+        "ka", ka, lambda p: perm_ref.at[1, most], lambda p: cond_all.at[y, x, p, most], (cond_s, cond_r)
+    )
     copies += send_all("pb", pb, lambda p: pack_ref, lambda p: rows_ref.at[p], (row_s, row_r))
     sibling = {"pb": pb + 1 - 2 * core}
     w_send = send_one(
@@ -160,6 +172,45 @@
     )
     copies += [w_send]
     copies += send_all("pb", pb, lambda p: val_all.at[pb], lambda p: val_all.at[p], (val_s, val_r))
+
+    parts = [lax.rem(x + o, 4) for o in (0, 3, 1, 2)]
+    for o, other in enumerate(chips):
+        recv_one(cond_all.at[other // 4, lax.rem(other, 4), ka, few], few_s.at[o], few_r.at[other], at(other))
+
+    def send_far(part):
+        return send_all(
+            "ka", ka,
+            lambda p: cond_all.at[:, part, ka, few],
+            lambda p: cond_all.at[:, part, p, few],
+            (far_s.at[part], far_r.at[part]),
+        )
+
+    copies += send_far(parts[0])
+
+    recv_all("ka", ka, lambda p: cond_all.at[y, x, p, most], (cond_s, cond_r))
+    lower = pl.ds(0, 8)
+    upper = pl.ds(8, 8)
+    across = (1 - y) * 4 + x
+    steps = [lax.rem(x + o, 4) for o in range(1, 4)]
+    block = cond_all.at[y, x, :, most]
+    copies += [send_one(block, block, hop_s.at[0], hop_r.at[0], at(across))]
+    for o in (0, 2, 1):
+        for first, which in ((1, upper), (10, lower)):
+            block = cond_all.at[y, x, which, most]
+            copies += [send_one(block, block, hop_s.at[first + o], hop_r.at[first + o], at(y * 4 + steps[o]))]
+
+    recv_all("pb", pb, lambda p: rows_ref.at[p], (row_s, row_r))
+    for i in range(N):
+        drow_ref[2 * i : 2 * i + 2, :] = rows_ref[i, 0]
+        erow_ref[2 * i : 2 * i + 2, :] = rows_ref[i, 1]
+    drow = drow_ref[...]
+    msg_ref[0, 0:32, :] = drow.astype(BF16)
+    msg_ref[0, 32:48, :] = stat_rows([total(drow * drow)])
+    dips_ref[ka] = msg_ref[0]
+    copies += send_all("ka", ka, lambda p: msg_ref.at[0], lambda p: dips_ref.at[p], (dip_s, dip_r))
+
+    for part in parts[1:]:
+        copies += send_far(part)
 
     def table(k):
         mine = grid_ref[k]
@@ -175,30 +226,6 @@
 
     loop(N, table)
 
-    recv_all("pb", pb, lambda p: rows_ref.at[p], (row_s, row_r))
-    for i in range(N):
-        drow_ref[2 * i : 2 * i + 2, :] = rows_ref[i, 0]
-        erow_ref[2 * i : 2 * i + 2, :] = rows_ref[i, 1]
-    drow = drow_ref[...]
-    msg_ref[0, 0:32, :] = drow.astype(BF16)
-    msg_ref[0, 32:48, :] = stat_rows([total(drow * drow)])
-    dips_ref[ka] = msg_ref[0]
-    copies += send_all("ka", ka, lambda p: msg_ref.at[0], lambda p: dips_ref.at[p], (dip_s, dip_r))
-
-    recv_all("ka", ka, lambda p: cond_all.at[chip, p], (cond_s, cond_r))
-    lower = pl.ds(0, 8)
-    upper = pl.ds(8, 8)
-    x_chips = [y * 4 + lax.rem(x + o, 4) for o in range(1, 4)]
-
-    def at(which):
-        return {"pb": which * 2 + core}
-
-    copies += [send_one(cond_all.at[chip], cond_all.at[chip], hop_s.at[0], hop_r.at[0], at(across))]
-    for o in range(3):
-        copies += [
-            send_one(cond_all.at[chip], cond_all.at[chip], hop_s.at[1 + o], hop_r.at[1 + o], at(x_chips[o]))
-        ]
-
     def turn(q):
         for j in range(8):
             wt_ref[j % 4, q, :, j // 4 * 128 : j // 4 * 128 + 128] = stage_ref[q, j].T
@@ -230,7 +257,7 @@
             sum_ref[k] = jnp.zeros((64, 128), F32)
 
     def columns(part, k):
-        return jnp.concatenate([cond_all[part, k], cond_all[part + 4, k]], axis=1)
+        return jnp.concatenate([cond_all[0, part, k], cond_all[1, part, k]], axis=1)
 
     def apply_part(part):
         def screen(k):
@@ -256,28 +283,28 @@
             ).astype(BF16)
 
     start_apply(dips_ref)
-    recv_one(cond_all.at[across], hop_s.at[0], hop_r.at[0], at(across))
+    recv_one(cond_all.at[1 - y, x, :, most], hop_s.at[0], hop_r.at[0], at(across))
+    block = cond_all.at[1 - y, x, lower, most]
     for o in range(3):
-        copies.append(
-            send_one(
-                cond_all.at[across, lower], cond_all.at[across, lower], hop_s.at[4 + o], hop_r.at[4 + o], at(x_chips[o])
-            )
-        )
-    apply_part(x)
-    for o in (0, 2, 1):
-        back = x_chips[2 - o]
-        recv_one(cond_all.at[back], hop_s.at[1 + o], hop_r.at[1 + o], at(back))
-        copies.append(
-            send_one(
-                cond_all.at[back, upper], cond_all.at[back, upper], hop_s.at[7 + o], hop_r.at[7 + o], at(across)
-            )
-        )
-    for o in (0, 2, 1):
-        back = x_chips[2 - o]
-        far = (1 - y) * 4 + lax.rem(back, 4)
-        recv_one(cond_all.at[far, lower], hop_s.at[4 + o], hop_r.at[4 + o], at(back))
-        recv_one(cond_all.at[far, upper], hop_s.at[7 + o], hop_r.at[7 + o], at(across))
-        apply_part(lax.rem(back, 4))
+        copies.append(send_one(block, block, hop_s.at[4 + o], hop_r.at[4 + o], at(y * 4 + steps[o])))
+
+    def recv_far(part):
+        recv_all("ka", ka, lambda p: cond_all.at[:, part, p, few], (far_s.at[part], far_r.at[part]))
+
+    for i, o in enumerate((0, 2, 1)):
+        back = parts[1 + i]
+        recv_one(cond_all.at[y, back, upper, most], hop_s.at[1 + o], hop_r.at[1 + o], at(y * 4 + back))
+        block = cond_all.at[y, back, upper, most]
+        copies.append(send_one(block, block, hop_s.at[7 + o], hop_r.at[7 + o], at(across)))
+    recv_far(parts[0])
+    apply_part(parts[0])
+    for i, o in enumerate((0, 2, 1)):
+        back = parts[1 + i]
+        recv_one(cond_all.at[y, back, lower, most], hop_s.at[10 + o], hop_r.at[10 + o], at(y * 4 + back))
+        recv_one(cond_all.at[1 - y, back, lower, most], hop_s.at[4 + o], hop_r.at[4 + o], at(y * 4 + back))
+        recv_one(cond_all.at[1 - y, back, upper, most], hop_s.at[7 + o], hop_r.at[7 + o], at(across))
+        recv_far(back)
+        apply_part(back)
     finish_apply(0)
 
     def reduce_rows(which):
@@ -345,9 +372,9 @@
     last = (rest - alpha * vector) / beta
     for i in range(N):
         cut_ref[i] = last[2 * i : 2 * i + 2, :]
-    u_out[...] = cut_ref[pb]
+    out_ref[0:2, :] = cut_ref[pb]
     lane = lax.broadcasted_iota(jnp.int32, (1, 128), 1)
-    coef_out[...] = jnp.where(
+    out_ref[2:3, :] = jnp.where(
         lane == 0, alpha_zero, jnp.where(lane == 1, alpha, jnp.where(lane == 2, beta_zero, beta))
     )
     for copy in copies:
@@ -360,14 +387,14 @@
     pair = [sem((N,)), sem((N,))]
     return pl.pallas_call(
         functools.partial(haydock_kernel, entries, factor),
-        out_shape=[jax.ShapeDtypeStruct((2, 128), F32), jax.ShapeDtypeStruct((1, 128), F32)],
-        in_specs=[pl.BlockSpec(memory_space=pl.ANY)] * 6,
-        out_specs=[vmem] * 2,
+        out_shape=jax.ShapeDtypeStruct((3, 128), F32),
+        in_specs=[pl.BlockSpec(memory_space=pltpu.HBM)] * 6,
+        out_specs=vmem,
         scratch_shapes=[
             pltpu.SMEM((N,), jnp.int32),
             pltpu.SMEM((N * N,), jnp.int32),
             pltpu.VMEM((2, 64, 128), BF16),
-            pltpu.VMEM((8, N, 64, 128), BF16),
+            pltpu.VMEM((2, 4, N, 64, 128), BF16),
             pltpu.VMEM((N, 64, 128), BF16),
             pltpu.VMEM((N, 256, 128), BF16),
             pltpu.VMEM((16, 8, 128, 128), BF16),
@@ -393,12 +420,14 @@
             pltpu.VMEM((N, 8, 128), F32),
             pltpu.VMEM((N, 2, 128), F32),
         ]
-        + pair * 5
+        + pair * 2
+        + [sem((4, N)), sem((4, N))]
+        + pair * 4
         + [sem((2,)), sem((6,))]
         + [sem((2, N))] * 4
         + pair * 2,
         compiler_params=pltpu.CompilerParams(
-            collective_id=0, has_side_effects=True, vmem_limit_bytes=48 * 1024 * 1024
+            collective_id=0, has_side_effects=True, vmem_limit_bytes=63 * 1024 * 1024
         ),
         name="haydock",
     )(*args)
@@ -407,7 +436,7 @@
 def per_device(dipole, energy, cond_amp, val_amp, screened, window):
     entries = 16 * 4096
     factor = 1.0 / (2048 * math.sqrt(entries))
-    out, coef = haydock(
+    out = haydock(
         entries,
         factor,
         window,
@@ -417,7 +446,7 @@
         val_amp[0],
         screened.reshape(8, 8, 2, 128, 128),
     )
-    return coef[0, :4], out.reshape(1, 256)
+    return out[2, :4], out[:2].reshape(1, 256)
 
 
 def solution(mesh):

time: 105 us -> 98.7 us (0.940)
  local copies, waits for them, and re-layouts: 6.7 us -> 2.44 us
  Pallas kernels: 97 us -> 95.4 us
    unnamed x13 -> x0, local copies, waits for them, and re-layouts: 6.19 us -> none
    pallas_call x1, Pallas kernels: 97 us -> 95.4 us  [haydock(): pl.pallas_call(functools.partial(haydock_kernel, entries, factor), out_sh...]
    slice x0 -> x1, local copies, waits for them, and re-layouts: none -> 1.24 us  [per_device(): return (out[2, :4], out[:2].reshape(1, 256))]
where the time goes in v4:
time: 98.7 us; the launch traced here: 98.5 us
  Pallas kernels  95.4 us (97%)
  local copies, waits for them, and re-layouts  2.44 us (2%)
    pallas_call x1, Pallas kernels, haydock(): pl.pallas_call(functools.partial(haydock_kernel, entries, factor), out_sh...  95.4 us

profile of v4, /device:TPU:1, one launch (start us, length us, event | category | flops | bytes accessed | tf_op | source)
XLA Modules:
  0.0 98.5 jit_solution(1334535171644078238)
XLA Ops:
  0.6 95.4 %haydock.1 = f32[3,128]{1,0:T(4,128)} custom-call(s32[16]{0:T(128)} %window_ref.1, f32[2,128]{1,0:T(2,128)} %bitcast.11, f32[2,128]{1,0:T(2,128)} %bitcast.12, bf16[64,128]{1,0:T(8,128)(2,1)} %bitcast.9, bf16[64,128]{1,0:T(8,128)(2,1)} %bitcast.10, bf16[8,8,2,128,128]{4,3,2,1,0:T(8,128)(2,1)} %bitcast.8), custom_call_target="tpu_custom_call" | custom-call | tf_op jit(solution)/shard_map/haydock/pallas_call | solution.py:388
  96.1 1.2 %slice_bitcast_fusion = f32[4]{0:T(128)} fusion(f32[3,128]{1,0:T(4,128)} %haydock.1), kind=kLoop, calls=%fused_computation | loop fusion | bytes 32 | tf_op jit(solution)/shard_map/squeeze | solution.py:449
  97.3 1.2 %slice.7 = f32[2,128]{1,0:T(2,128)} slice(f32[3,128]{1,0:T(4,128)} %haydock.1), slice={[0:2], [0:128]} | slice | bytes 2048 | tf_op jit(solution)/shard_map/slice | solution.py:449

commit v5 on v4

--- a/solution.py
+++ b/solution.py
@@ -86,15 +86,20 @@
 
 
 def pack(values):
-    row = lax.broadcasted_iota(jnp.int32, (8, 128), 0)
-    block = jnp.zeros((8, 128), F32)
+    lane = lax.broadcasted_iota(jnp.int32, (1, 128), 1)
+    block = jnp.zeros((1, 128), F32)
     for i, value in enumerate(values):
-        block = jnp.where(row == i, jnp.broadcast_to(value, (8, 128)), block)
+        block = jnp.where(lane == i, jnp.broadcast_to(value, (1, 128)), block)
     return block
 
 
 def safe_divide(top, bottom):
     return jnp.where(bottom > 0, top / jnp.where(bottom > 0, bottom, 1.0), 0.0)
+
+
+def drain(copies):
+    for copy in copies:
+        copy.wait_send()
 
 
 def loop(count, body):
@@ -113,7 +118,7 @@
     pack_ref, rows_ref, drow_ref, erow_ref, msg_ref, dips_ref, u_ref,
     half_ref, pair_ref, screen_ref, sum_ref, part_ref, first_ref, mine_ref, second_ref,
     after_ref, rests_ref, stat_ref, stats_ref, cut_ref,
-    row_s, row_r, few_s, few_r, far_s, far_r, cond_s, cond_r, val_s, val_r, dip_s, dip_r, hop_s, hop_r, w_sem, own_sem,
+    row_s, row_r, few_s, few_r, far_s, far_r, side_s, side_r, cond_s, cond_r, val_s, val_r, dip_s, dip_r, hop_s, hop_r, w_sem, own_sem,
     a_s, a_r, b_s, b_r, d_s, d_r, e_s, e_r,
 ):
     ka = lax.axis_index("ka")
@@ -121,9 +126,13 @@
     core = lax.rem(pb, 2)
     chip = pb // 2
     x = lax.rem(chip, 4)
+    z = ka // 2
+    side = lax.rem(ka, 2)
     y = chip // 4
     barrier = pltpu.get_barrier_semaphore()
     signal_all(barrier, ka, pb)
+    mirror = {"ka": ka + 1 - 2 * side, "pb": lax.rem(pb + 8, N)}
+    pl.semaphore_signal(barrier, inc=1, device_id=mirror, device_id_type=MESH)
 
     loads = [
         pltpu.make_async_copy(source, target, own_sem.at[1 + i])
@@ -147,9 +156,9 @@
     for load in loads:
         load.wait()
     perm_ref[1] = jnp.dot(pick, perm_ref[0], preferred_element_type=F32).astype(BF16)
-    cond_all[y, x, ka] = perm_ref[1]
+    cond_all[y, x, z, side] = perm_ref[1]
     rows_ref[pb] = pack_ref[...]
-    pl.semaphore_wait(barrier, 2 * (N - 1))
+    pl.semaphore_wait(barrier, 2 * (N - 1) + 1)
 
     most = pl.ds(0, 48)
     few = pl.ds(48, 16)
@@ -159,11 +168,11 @@
         return {"pb": which * 2 + core}
 
     copies = [
-        send_one(perm_ref.at[1, few], cond_all.at[y, x, ka, few], few_s.at[o], few_r.at[chip], at(other))
+        send_one(perm_ref.at[1, few], cond_all.at[y, x, z, side, few], few_s.at[o], few_r.at[chip], at(other))
         for o, other in enumerate(chips)
     ]
     copies += send_all(
-        "ka", ka, lambda p: perm_ref.at[1, most], lambda p: cond_all.at[y, x, p, most], (cond_s, cond_r)
+        "ka", ka, lambda p: perm_ref.at[1, most], lambda p: cond_all.at[y, x, p // 2, lax.rem(p, 2), most], (cond_s, cond_r)
     )
     copies += send_all("pb", pb, lambda p: pack_ref, lambda p: rows_ref.at[p], (row_s, row_r))
     sibling = {"pb": pb + 1 - 2 * core}
@@ -175,28 +184,36 @@
 
     parts = [lax.rem(x + o, 4) for o in (0, 3, 1, 2)]
     for o, other in enumerate(chips):
-        recv_one(cond_all.at[other // 4, lax.rem(other, 4), ka, few], few_s.at[o], few_r.at[other], at(other))
+        recv_one(cond_all.at[other // 4, lax.rem(other, 4), z, side, few], few_s.at[o], few_r.at[other], at(other))
+
+    beside = {"ka": ka + 1 - 2 * side}
+    columns_z = [lax.rem(z + o, 8) for o in range(1, 8)]
 
     def send_far(part):
-        return send_all(
-            "ka", ka,
-            lambda p: cond_all.at[:, part, ka, few],
-            lambda p: cond_all.at[:, part, p, few],
-            (far_s.at[part], far_r.at[part]),
-        )
+        block = cond_all.at[:, part, z, side, few]
+        return [
+            send_one(block, block, far_s.at[part, o], far_r.at[part, z], {"ka": other * 2 + side})
+            for o, other in enumerate(columns_z)
+        ]
+
+    def pass_far(part):
+        for o, other in enumerate(columns_z):
+            block = cond_all.at[:, part, other, side, few]
+            recv_one(block, far_s.at[part, o], far_r.at[part, other], {"ka": other * 2 + side})
+        block = cond_all.at[:, part, :, side, few]
+        return [send_one(block, block, side_s.at[part], side_r.at[part], beside)]
 
     copies += send_far(parts[0])
 
-    recv_all("ka", ka, lambda p: cond_all.at[y, x, p, most], (cond_s, cond_r))
-    lower = pl.ds(0, 8)
-    upper = pl.ds(8, 8)
-    across = (1 - y) * 4 + x
+    recv_all("ka", ka, lambda p: cond_all.at[y, x, p // 2, lax.rem(p, 2), most], (cond_s, cond_r))
+    lower = pl.ds(0, 4)
+    upper = pl.ds(4, 4)
     steps = [lax.rem(x + o, 4) for o in range(1, 4)]
-    block = cond_all.at[y, x, :, most]
-    copies += [send_one(block, block, hop_s.at[0], hop_r.at[0], at(across))]
+    block = cond_all.at[y, x, :, :, most]
+    copies += [send_one(block, block, hop_s.at[0], hop_r.at[0], mirror)]
     for o in (0, 2, 1):
         for first, which in ((1, upper), (10, lower)):
-            block = cond_all.at[y, x, which, most]
+            block = cond_all.at[y, x, which, :, most]
             copies += [send_one(block, block, hop_s.at[first + o], hop_r.at[first + o], at(y * 4 + steps[o]))]
 
     recv_all("pb", pb, lambda p: rows_ref.at[p], (row_s, row_r))
@@ -257,18 +274,23 @@
             sum_ref[k] = jnp.zeros((64, 128), F32)
 
     def columns(part, k):
-        return jnp.concatenate([cond_all[0, part, k], cond_all[1, part, k]], axis=1)
+        return jnp.concatenate([cond_all[0, part, k // 2, k % 2], cond_all[1, part, k // 2, k % 2]], axis=1)
 
     def apply_part(part):
-        def screen(k):
-            acc = jnp.zeros((128, 256), BF16)
-            for other in range(N):
-                acc = acc + wt_ref[part, index_ref[k * N + other]] * pair_ref[other]
-            screen_ref[k] = acc
+        def screen(g):
+            for top in (0, 64):
+                rows = slice(top, top + 64)
+                accs = [jnp.zeros((64, 256), BF16)] * 4
+                for other in range(N):
+                    pair = pair_ref[other, rows, :]
+                    for i in range(4):
+                        accs[i] = accs[i] + wt_ref[part, index_ref[(g * 4 + i) * N + other], rows, :] * pair
+                for i in range(4):
+                    screen_ref[g * 4 + i, rows, :] = accs[i]
 
         for k in range(N):
             pair_ref[k] = jnp.dot(half_ref[k], columns(part, k), preferred_element_type=F32).astype(BF16)
-        loop(N, screen)
+        loop(N // 4, screen)
         for k in range(N):
             sum_ref[k] += lax.dot_general(columns(part, k), screen_ref[k], NT, preferred_element_type=F32)
 
@@ -283,46 +305,51 @@
             ).astype(BF16)
 
     start_apply(dips_ref)
-    recv_one(cond_all.at[1 - y, x, :, most], hop_s.at[0], hop_r.at[0], at(across))
-    block = cond_all.at[1 - y, x, lower, most]
+    for part in parts[:2]:
+        copies += pass_far(part)
+    recv_one(cond_all.at[1 - y, x, :, :, most], hop_s.at[0], hop_r.at[0], mirror)
+    block = cond_all.at[1 - y, x, lower, :, most]
     for o in range(3):
         copies.append(send_one(block, block, hop_s.at[4 + o], hop_r.at[4 + o], at(y * 4 + steps[o])))
 
     def recv_far(part):
-        recv_all("ka", ka, lambda p: cond_all.at[:, part, p, few], (far_s.at[part], far_r.at[part]))
+        recv_one(cond_all.at[:, part, :, 1 - side, few], side_s.at[part], side_r.at[part], beside)
 
     for i, o in enumerate((0, 2, 1)):
-        back = parts[1 + i]
-        recv_one(cond_all.at[y, back, upper, most], hop_s.at[1 + o], hop_r.at[1 + o], at(y * 4 + back))
-        block = cond_all.at[y, back, upper, most]
-        copies.append(send_one(block, block, hop_s.at[7 + o], hop_r.at[7 + o], at(across)))
+        near = parts[1 + i]
+        recv_one(cond_all.at[y, near, upper, :, most], hop_s.at[1 + o], hop_r.at[1 + o], at(y * 4 + near))
+        block = cond_all.at[y, near, upper, :, most]
+        copies.append(send_one(block, block, hop_s.at[7 + o], hop_r.at[7 + o], mirror))
+    for part in parts[2:]:
+        copies += pass_far(part)
     recv_far(parts[0])
     apply_part(parts[0])
     for i, o in enumerate((0, 2, 1)):
-        back = parts[1 + i]
-        recv_one(cond_all.at[y, back, lower, most], hop_s.at[10 + o], hop_r.at[10 + o], at(y * 4 + back))
-        recv_one(cond_all.at[1 - y, back, lower, most], hop_s.at[4 + o], hop_r.at[4 + o], at(y * 4 + back))
-        recv_one(cond_all.at[1 - y, back, upper, most], hop_s.at[7 + o], hop_r.at[7 + o], at(across))
-        recv_far(back)
-        apply_part(back)
+        near = parts[1 + i]
+        recv_one(cond_all.at[y, near, lower, :, most], hop_s.at[10 + o], hop_r.at[10 + o], at(y * 4 + near))
+        recv_one(cond_all.at[1 - y, near, lower, :, most], hop_s.at[4 + o], hop_r.at[4 + o], at(y * 4 + near))
+        recv_one(cond_all.at[1 - y, near, upper, :, most], hop_s.at[7 + o], hop_r.at[7 + o], mirror)
+        recv_far(near)
+        apply_part(near)
     finish_apply(0)
 
-    def reduce_rows(which):
+    def reduce_rows(which, before):
         new = send_all(
             "ka", ka, lambda p: part_ref.at[which, p], lambda p: first_ref.at[which, p], (a_s.at[which], a_r.at[which])
         )
         first_ref[which, ka] = part_ref[which, ka]
+        drain(before)
         recv_all("ka", ka, lambda p: first_ref.at[which, p], (a_s.at[which], a_r.at[which]))
         mine_ref[which] = jnp.sum(first_ref[which].astype(F32), axis=0).astype(BF16)
         second_ref[which, pb] = mine_ref[which]
-        new += send_all(
+        last = send_all(
             "pb", pb, lambda p: mine_ref.at[which], lambda p: second_ref.at[which, p], (b_s.at[which], b_r.at[which])
         )
+        drain(new)
         recv_all("pb", pb, lambda p: second_ref.at[which, p], (b_s.at[which], b_r.at[which]))
-        return jnp.sum(second_ref[which].astype(F32), axis=0), new
-
-    kernel_row, new = reduce_rows(0)
-    copies += new
+        return jnp.sum(second_ref[which].astype(F32), axis=0), last
+
+    kernel_row, copies = reduce_rows(0, copies)
     squares = read_stat(dips_ref[:, 32:48, :].astype(F32), 0)
     scale = 1.0 / jnp.sqrt(jnp.sum(squares, axis=0) / entries + EPSILON)
     vector = drow_ref[...] * scale
@@ -350,10 +377,10 @@
     after_ref[1] = (image - alpha_zero * vector) / beta_zero
 
     start_apply(u_ref)
-    loop(4, apply_part)
+    for part in range(4):
+        apply_part(part)
     finish_apply(1)
-    kernel_row, new = reduce_rows(1)
-    copies += new
+    kernel_row, copies = reduce_rows(1, copies)
     former = after_ref[0]
     vector = after_ref[1]
     image = erow_ref[...] * vector - factor / beta_zero * kernel_row
@@ -363,9 +390,13 @@
     gap = rest - slope * vector
     stat_ref[...] = pack([total(vector * image), slope, total(gap * gap), norm])
     stats_ref[ka] = stat_ref[...]
-    copies += send_all("ka", ka, lambda p: stat_ref, lambda p: stats_ref.at[p], (e_s, e_r))
+    final = send_all("ka", ka, lambda p: stat_ref, lambda p: stats_ref.at[p], (e_s, e_r))
+    drain(copies)
     recv_all("ka", ka, lambda p: stats_ref.at[p], (e_s, e_r))
-    inners, slopes, lefts, norms = [stats_ref[:, i : i + 1, :] for i in range(4)]
+    stats = stats_ref[...]
+    inners, slopes, lefts, norms = [
+        jnp.broadcast_to(stats[:, :, i : i + 1], (N, 1, 128)) for i in range(4)
+    ]
     alpha = jnp.sum(inners, axis=0) / entries
     off = slopes - alpha
     beta = jnp.sqrt(jnp.sum(lefts + norms * off * off, axis=0) / entries + EPSILON)
@@ -377,8 +408,7 @@
     out_ref[2:3, :] = jnp.where(
         lane == 0, alpha_zero, jnp.where(lane == 1, alpha, jnp.where(lane == 2, beta_zero, beta))
     )
-    for copy in copies:
-        copy.wait_send()
+    drain(final)
 
 
 def haydock(entries, factor, *args):
@@ -394,7 +424,7 @@
             pltpu.SMEM((N,), jnp.int32),
             pltpu.SMEM((N * N,), jnp.int32),
             pltpu.VMEM((2, 64, 128), BF16),
-            pltpu.VMEM((2, 4, N, 64, 128), BF16),
+            pltpu.VMEM((2, 4, 8, 2, 64, 128), BF16),
             pltpu.VMEM((N, 64, 128), BF16),
             pltpu.VMEM((N, 256, 128), BF16),
             pltpu.VMEM((16, 8, 128, 128), BF16),
@@ -416,12 +446,12 @@
             pltpu.VMEM((2, N, 32, 128), BF16),
             pltpu.VMEM((2, 32, 128), F32),
             pltpu.VMEM((N, 48, 128), BF16),
-            pltpu.VMEM((8, 128), F32),
-            pltpu.VMEM((N, 8, 128), F32),
+            pltpu.VMEM((1, 128), F32),
+            pltpu.VMEM((N, 1, 128), F32),
             pltpu.VMEM((N, 2, 128), F32),
         ]
         + pair * 2
-        + [sem((4, N)), sem((4, N))]
+        + [sem((4, N)), sem((4, N)), sem((4,)), sem((4,))]
         + pair * 4
         + [sem((2,)), sem((6,))]
         + [sem((2, N))] * 4

time: 98.7 us -> 94.7 us (0.959)
  Pallas kernels: 95.4 us -> 91.4 us
    pallas_call x1, Pallas kernels: 95.4 us -> 91.4 us  [haydock(): pl.pallas_call(functools.partial(haydock_kernel, entries, factor), out_sh...]
where the time goes in v5:
time: 94.7 us; the launch traced here: 94.4 us
  Pallas kernels  91.4 us (97%)
  local copies, waits for them, and re-layouts  2.44 us (3%)
    pallas_call x1, Pallas kernels, haydock(): pl.pallas_call(functools.partial(haydock_kernel, entries, factor), out_sh...  91.4 us

profile of v5, /device:TPU:1, one launch (start us, length us, event | category | flops | bytes accessed | tf_op | source)
XLA Modules:
  0.0 94.4 jit_solution(5123435102891347857)
XLA Ops:
  0.6 91.4 %haydock.1 = f32[3,128]{1,0:T(4,128)} custom-call(s32[16]{0:T(128)} %window_ref.1, f32[2,128]{1,0:T(2,128)} %bitcast.11, f32[2,128]{1,0:T(2,128)} %bitcast.12, bf16[64,128]{1,0:T(8,128)(2,1)} %bitcast.9, bf16[64,128]{1,0:T(8,128)(2,1)} %bitcast.10, bf16[8,8,2,128,128]{4,3,2,1,0:T(8,128)(2,1)} %bitcast.8), custom_call_target="tpu_custom_call" | custom-call | tf_op jit(solution)/shard_map/haydock/pallas_call | solution.py:418
  92.0 1.2 %slice_bitcast_fusion = f32[4]{0:T(128)} fusion(f32[3,128]{1,0:T(4,128)} %haydock.1), kind=kLoop, calls=%fused_computation | loop fusion | bytes 32 | tf_op jit(solution)/shard_map/squeeze | solution.py:479
  93.2 1.2 %slice.7 = f32[2,128]{1,0:T(2,128)} slice(f32[3,128]{1,0:T(4,128)} %haydock.1), slice={[0:2], [0:128]} | slice | bytes 2048 | tf_op jit(solution)/shard_map/slice | solution.py:479

commit v6 on v5

--- a/solution.py
+++ b/solution.py
@@ -158,77 +158,6 @@
     perm_ref[1] = jnp.dot(pick, perm_ref[0], preferred_element_type=F32).astype(BF16)
     cond_all[y, x, z, side] = perm_ref[1]
     rows_ref[pb] = pack_ref[...]
-    pl.semaphore_wait(barrier, 2 * (N - 1) + 1)
-
-    most = pl.ds(0, 48)
-    few = pl.ds(48, 16)
-    chips = [lax.rem(chip + o, 8) for o in range(1, 8)]
-
-    def at(which):
-        return {"pb": which * 2 + core}
-
-    copies = [
-        send_one(perm_ref.at[1, few], cond_all.at[y, x, z, side, few], few_s.at[o], few_r.at[chip], at(other))
-        for o, other in enumerate(chips)
-    ]
-    copies += send_all(
-        "ka", ka, lambda p: perm_ref.at[1, most], lambda p: cond_all.at[y, x, p // 2, lax.rem(p, 2), most], (cond_s, cond_r)
-    )
-    copies += send_all("pb", pb, lambda p: pack_ref, lambda p: rows_ref.at[p], (row_s, row_r))
-    sibling = {"pb": pb + 1 - 2 * core}
-    w_send = send_one(
-        w_ref.at[:, :, 1 - core], stage_ref.at[pl.ds(core * 8, 8)], w_sem.at[0], w_sem.at[1], sibling
-    )
-    copies += [w_send]
-    copies += send_all("pb", pb, lambda p: val_all.at[pb], lambda p: val_all.at[p], (val_s, val_r))
-
-    parts = [lax.rem(x + o, 4) for o in (0, 3, 1, 2)]
-    for o, other in enumerate(chips):
-        recv_one(cond_all.at[other // 4, lax.rem(other, 4), z, side, few], few_s.at[o], few_r.at[other], at(other))
-
-    beside = {"ka": ka + 1 - 2 * side}
-    columns_z = [lax.rem(z + o, 8) for o in range(1, 8)]
-
-    def send_far(part):
-        block = cond_all.at[:, part, z, side, few]
-        return [
-            send_one(block, block, far_s.at[part, o], far_r.at[part, z], {"ka": other * 2 + side})
-            for o, other in enumerate(columns_z)
-        ]
-
-    def pass_far(part):
-        for o, other in enumerate(columns_z):
-            block = cond_all.at[:, part, other, side, few]
-            recv_one(block, far_s.at[part, o], far_r.at[part, other], {"ka": other * 2 + side})
-        block = cond_all.at[:, part, :, side, few]
-        return [send_one(block, block, side_s.at[part], side_r.at[part], beside)]
-
-    copies += send_far(parts[0])
-
-    recv_all("ka", ka, lambda p: cond_all.at[y, x, p // 2, lax.rem(p, 2), most], (cond_s, cond_r))
-    lower = pl.ds(0, 4)
-    upper = pl.ds(4, 4)
-    steps = [lax.rem(x + o, 4) for o in range(1, 4)]
-    block = cond_all.at[y, x, :, :, most]
-    copies += [send_one(block, block, hop_s.at[0], hop_r.at[0], mirror)]
-    for o in (0, 2, 1):
-        for first, which in ((1, upper), (10, lower)):
-            block = cond_all.at[y, x, which, :, most]
-            copies += [send_one(block, block, hop_s.at[first + o], hop_r.at[first + o], at(y * 4 + steps[o]))]
-
-    recv_all("pb", pb, lambda p: rows_ref.at[p], (row_s, row_r))
-    for i in range(N):
-        drow_ref[2 * i : 2 * i + 2, :] = rows_ref[i, 0]
-        erow_ref[2 * i : 2 * i + 2, :] = rows_ref[i, 1]
-    drow = drow_ref[...]
-    msg_ref[0, 0:32, :] = drow.astype(BF16)
-    msg_ref[0, 32:48, :] = stat_rows([total(drow * drow)])
-    dips_ref[ka] = msg_ref[0]
-    copies += send_all("ka", ka, lambda p: msg_ref.at[0], lambda p: dips_ref.at[p], (dip_s, dip_r))
-
-    for part in parts[1:]:
-        copies += send_far(part)
-
     def table(k):
         mine = grid_ref[k]
         for other in range(N):
@@ -242,7 +171,6 @@
             )
 
     loop(N, table)
-
     def turn(q):
         for j in range(8):
             wt_ref[j % 4, q, :, j // 4 * 128 : j // 4 * 128 + 128] = stage_ref[q, j].T
@@ -251,9 +179,86 @@
     loop(8, lambda q: turn(core * 8 + q))
     for i in range(4):
         wt_ref[i, 16] = jnp.zeros((128, 256), BF16)
+    pl.semaphore_wait(barrier, 2 * (N - 1) + 1)
+
+    most = pl.ds(0, 48)
+    few = pl.ds(48, 16)
+    chips = [lax.rem(chip + o, 8) for o in range(1, 8)]
+
+    def at(which):
+        return {"pb": which * 2 + core}
+
+    copies = [
+        send_one(perm_ref.at[1, few], cond_all.at[y, x, z, side, few], few_s.at[o], few_r.at[chip], at(other))
+        for o, other in enumerate(chips)
+    ]
+    copies += send_all(
+        "ka", ka, lambda p: perm_ref.at[1, most], lambda p: cond_all.at[y, x, p // 2, lax.rem(p, 2), most], (cond_s, cond_r)
+    )
+    copies += send_all("pb", pb, lambda p: pack_ref, lambda p: rows_ref.at[p], (row_s, row_r))
+    sibling = {"pb": pb + 1 - 2 * core}
+    w_send = send_one(
+        w_ref.at[:, :, 1 - core], stage_ref.at[pl.ds(core * 8, 8)], w_sem.at[0], w_sem.at[1], sibling
+    )
+    copies += [w_send]
+    copies += send_all("pb", pb, lambda p: val_all.at[pb], lambda p: val_all.at[p], (val_s, val_r))
+
+    parts = [lax.rem(x + o, 4) for o in (0, 3, 1, 2)]
+    for o, other in enumerate(chips):
+        recv_one(cond_all.at[other // 4, lax.rem(other, 4), z, side, few], few_s.at[o], few_r.at[other], at(other))
+
+    beside = {"ka": ka + 1 - 2 * side}
+    columns_z = [lax.rem(z + o, 8) for o in range(1, 8)]
+
+    def send_far(part):
+        block = cond_all.at[:, part, z, side, few]
+        return [
+            send_one(block, block, far_s.at[part, o], far_r.at[part, z], {"ka": other * 2 + side})
+            for o, other in enumerate(columns_z)
+        ]
+
+    def pass_far(part):
+        for o, other in enumerate(columns_z):
+            block = cond_all.at[:, part, other, side, few]
+            recv_one(block, far_s.at[part, o], far_r.at[part, other], {"ka": other * 2 + side})
+        block = cond_all.at[:, part, :, side, few]
+        return [send_one(block, block, side_s.at[part], side_r.at[part], beside)]
+
+    for part in parts:
+        copies += send_far(part)
+
+    recv_all("ka", ka, lambda p: cond_all.at[y, x, p // 2, lax.rem(p, 2), most], (cond_s, cond_r))
+    lower = pl.ds(0, 4)
+    upper = pl.ds(4, 4)
+    steps = [lax.rem(x + o, 4) for o in range(1, 4)]
+    block = cond_all.at[y, x, :, :, most]
+    copies += [send_one(block, block, hop_s.at[0], hop_r.at[0], mirror)]
+    for o, slot, which in ((0, 1, upper), (2, 12, lower), (0, 10, lower), (2, 3, upper)):
+        block = cond_all.at[y, x, which, :, most]
+        copies += [send_one(block, block, hop_s.at[slot], hop_r.at[slot], at(y * 4 + steps[o]))]
+
+    recv_all("pb", pb, lambda p: rows_ref.at[p], (row_s, row_r))
+    for i in range(N):
+        drow_ref[2 * i : 2 * i + 2, :] = rows_ref[i, 0]
+        erow_ref[2 * i : 2 * i + 2, :] = rows_ref[i, 1]
+    drow = drow_ref[...]
+    msg_ref[0, 0:32, :] = drow.astype(BF16)
+    msg_ref[0, 32:48, :] = stat_rows([total(drow * drow)])
+    dips_ref[ka] = msg_ref[0]
+    copies += send_all("ka", ka, lambda p: msg_ref.at[0], lambda p: dips_ref.at[p], (dip_s, dip_r))
+
+    for o, slot, which, onward in ((0, 1, upper, 2), (2, 12, lower, 11)):
+        near = steps[2 - o]
+        block = cond_all.at[y, near, which, :, most]
+        recv_one(block, hop_s.at[slot], hop_r.at[slot], at(y * 4 + near))
+        copies += [send_one(block, block, hop_s.at[onward], hop_r.at[onward], at(y * 4 + steps[o]))]
+
+
     recv_one(stage_ref.at[pl.ds((1 - core) * 8, 8)], w_sem.at[0], w_sem.at[1], sibling)
     loop(8, lambda q: turn((1 - core) * 8 + q))
 
+    for part in parts:
+        copies += pass_far(part)
     recv_all("pb", pb, lambda p: val_all.at[p], (val_s, val_r))
 
     def spread(k):
@@ -290,7 +295,8 @@
 
         for k in range(N):
             pair_ref[k] = jnp.dot(half_ref[k], columns(part, k), preferred_element_type=F32).astype(BF16)
-        loop(N // 4, screen)
+        for g in range(N // 4):
+            screen(g)
         for k in range(N):
             sum_ref[k] += lax.dot_general(columns(part, k), screen_ref[k], NT, preferred_element_type=F32)
 
@@ -305,8 +311,6 @@
             ).astype(BF16)
 
     start_apply(dips_ref)
-    for part in parts[:2]:
-        copies += pass_far(part)
     recv_one(cond_all.at[1 - y, x, :, :, most], hop_s.at[0], hop_r.at[0], mirror)
     block = cond_all.at[1 - y, x, lower, :, most]
     for o in range(3):
@@ -317,16 +321,16 @@
 
     for i, o in enumerate((0, 2, 1)):
         near = parts[1 + i]
-        recv_one(cond_all.at[y, near, upper, :, most], hop_s.at[1 + o], hop_r.at[1 + o], at(y * 4 + near))
+        if o != 0:
+            recv_one(cond_all.at[y, near, upper, :, most], hop_s.at[1 + o], hop_r.at[1 + o], at(y * 4 + near))
         block = cond_all.at[y, near, upper, :, most]
         copies.append(send_one(block, block, hop_s.at[7 + o], hop_r.at[7 + o], mirror))
-    for part in parts[2:]:
-        copies += pass_far(part)
     recv_far(parts[0])
     apply_part(parts[0])
     for i, o in enumerate((0, 2, 1)):
         near = parts[1 + i]
-        recv_one(cond_all.at[y, near, lower, :, most], hop_s.at[10 + o], hop_r.at[10 + o], at(y * 4 + near))
+        if o != 2:
+            recv_one(cond_all.at[y, near, lower, :, most], hop_s.at[10 + o], hop_r.at[10 + o], at(y * 4 + near))
         recv_one(cond_all.at[1 - y, near, lower, :, most], hop_s.at[4 + o], hop_r.at[4 + o], at(y * 4 + near))
         recv_one(cond_all.at[1 - y, near, upper, :, most], hop_s.at[7 + o], hop_r.at[7 + o], mirror)
         recv_far(near)

time: 94.7 us -> 90.5 us (0.956)
  Pallas kernels: 91.4 us -> 87.2 us
    pallas_call x1, Pallas kernels: 91.4 us -> 87.2 us  [haydock(): pl.pallas_call(functools.partial(haydock_kernel, entries, factor), out_sh...]
where the time goes in v6:
time: 90.5 us; the launch traced here: 90.3 us
  Pallas kernels  87.2 us (96%)
  local copies, waits for them, and re-layouts  2.44 us (3%)
    pallas_call x1, Pallas kernels, haydock(): pl.pallas_call(functools.partial(haydock_kernel, entries, factor), out_sh...  87.2 us

profile of v6, /device:TPU:1, one launch (start us, length us, event | category | flops | bytes accessed | tf_op | source)
XLA Modules:
  0.0 90.3 jit_solution(7517301823377913484)
XLA Ops:
  0.6 87.2 %haydock.1 = f32[3,128]{1,0:T(4,128)} custom-call(s32[16]{0:T(128)} %window_ref.1, f32[2,128]{1,0:T(2,128)} %bitcast.11, f32[2,128]{1,0:T(2,128)} %bitcast.12, bf16[64,128]{1,0:T(8,128)(2,1)} %bitcast.9, bf16[64,128]{1,0:T(8,128)(2,1)} %bitcast.10, bf16[8,8,2,128,128]{4,3,2,1,0:T(8,128)(2,1)} %bitcast.8), custom_call_target="tpu_custom_call" | custom-call | tf_op jit(solution)/shard_map/haydock/pallas_call | solution.py:422
  87.9 1.2 %slice_bitcast_fusion = f32[4]{0:T(128)} fusion(f32[3,128]{1,0:T(4,128)} %haydock.1), kind=kLoop, calls=%fused_computation | loop fusion | bytes 32 | tf_op jit(solution)/shard_map/squeeze | solution.py:483
  89.1 1.2 %slice.7 = f32[2,128]{1,0:T(2,128)} slice(f32[3,128]{1,0:T(4,128)} %haydock.1), slice={[0:2], [0:128]} | slice | bytes 2048 | tf_op jit(solution)/shard_map/slice | solution.py:483

commit v7 on v6

--- a/solution.py
+++ b/solution.py
@@ -268,7 +268,8 @@
             [jnp.concatenate([turned, zero], axis=1), jnp.concatenate([zero, turned], axis=1)], axis=0
         )
 
-    loop(N, spread)
+    for k in range(N):
+        spread(k)
     recv_all("ka", ka, lambda p: dips_ref.at[p], (dip_s, dip_r))
 
     def start_apply(vector_ref):

time: 90.5 us -> 90 us (level)
  no operation moved by 1% of the time
where the time goes in v7:
time: 90 us; the launch traced here: 89.7 us
  Pallas kernels  86.7 us (96%)
  local copies, waits for them, and re-layouts  2.44 us (3%)
    pallas_call x1, Pallas kernels, haydock(): pl.pallas_call(functools.partial(haydock_kernel, entries, factor), out_sh...  86.7 us

profile of v7, /device:TPU:1, one launch (start us, length us, event | category | flops | bytes accessed | tf_op | source)
XLA Modules:
  0.0 89.7 jit_solution(5971957890791904441)
XLA Ops:
  0.6 86.7 %haydock.1 = f32[3,128]{1,0:T(4,128)} custom-call(s32[16]{0:T(128)} %window_ref.1, f32[2,128]{1,0:T(2,128)} %bitcast.11, f32[2,128]{1,0:T(2,128)} %bitcast.12, bf16[64,128]{1,0:T(8,128)(2,1)} %bitcast.9, bf16[64,128]{1,0:T(8,128)(2,1)} %bitcast.10, bf16[8,8,2,128,128]{4,3,2,1,0:T(8,128)(2,1)} %bitcast.8), custom_call_target="tpu_custom_call" | custom-call | tf_op jit(solution)/shard_map/haydock/pallas_call | solution.py:423
  87.3 1.2 %slice_bitcast_fusion = f32[4]{0:T(128)} fusion(f32[3,128]{1,0:T(4,128)} %haydock.1), kind=kLoop, calls=%fused_computation | loop fusion | bytes 32 | tf_op jit(solution)/shard_map/squeeze | solution.py:484
  88.5 1.2 %slice.7 = f32[2,128]{1,0:T(2,128)} slice(f32[3,128]{1,0:T(4,128)} %haydock.1), slice={[0:2], [0:128]} | slice | bytes 2048 | tf_op jit(solution)/shard_map/slice | solution.py:484
